TPU v7x, 512 devices: a whole 4x4x16 slice. The times are simulated.
512 devices in a mesh: ctx: 32 (over z_lo, y), head: 16 (over z_hi, x, core).
Axes of the slice: x: 4, y: 4, z: 16 (z_hi: 2, z_lo: 8; z = z_hi * 8 + z_lo), core: 2. Of those that a mesh axis runs over, the one named last changes fastest.
Arguments:
- query_latent: bfloat16 [4096, 128, 512], P('ctx', 'head'), may hold values from -156 to 156
- query_rope: bfloat16 [4096, 8192], P('ctx', 'head'), may hold values from -4.1875 to 4.1875
- latent: bfloat16 [4096, 512], P('ctx'), may hold values from -8 to 8
- key_rope: bfloat16 [4096, 64], P('ctx'), may hold values from -6 to 6
- doc_ids: int32 [4096], P('ctx'), may hold values from 0 to 31, never falling along the last dimension, each value on 1 to 512 neighbouring positions
- grad_out: bfloat16 [4096, 128, 512], P('ctx', 'head'), may hold values from -6 to 6
Outputs:
- attended: bfloat16 [4096, 128, 512], P('ctx', 'head')
- grad_query_latent: bfloat16 [4096, 128, 512], P('ctx', 'head')
- grad_query_rope: bfloat16 [4096, 8192], P('ctx', 'head')
- grad_latent: float32 [4096, 512], P('ctx')
- grad_key_rope: float32 [4096, 64], P('ctx')
Inputs may be any that keep to these rules, and one draw needn't show every extreme that they name: `doc_ids`: document ids never fall along the tokens; every document has 1 to 512 tokens and one has exactly 512.
All inputs are finite; a program needn't handle non-finite values.
Results may differ from a plain program's by a relative error of at most 0.01.
Values may be sent and summed in bfloat16 or wider, within the bound.
A program may use at most 128 MiB of HBM per device.

v0:
```python
from functools import reduce

import jax
import jax.numpy as jnp
from jax import lax
from jax.sharding import PartitionSpec as P

score_scale = 192.0 ** (-0.5)
negative = -1e30


def from_behind(x, axis, by):
    devices = lax.axis_size(axis)
    pairs = [(i, i + by) for i in range(devices) if 0 <= i + by < devices]
    return lax.ppermute(x, axis, pairs)


def per_device(query_latent, query_rope, latent, key_rope, doc_ids, grad_out):
    row_count, head_count, latent_width = query_latent.shape
    rope_width = key_rope.shape[1]
    rope_heads = query_rope.reshape(row_count, head_count, rope_width)
    reach_back = lax.axis_size("ctx") // 8
    own_index = lax.axis_index("ctx")
    offsets = jnp.arange(row_count, dtype=jnp.int32)
    query_pos = own_index * row_count + offsets
    sources = []
    for distance in range(reach_back, 0, -1):
        arrived = from_behind((latent, key_rope, doc_ids), "ctx", distance)
        sources.append((distance, arrived[0], arrived[1], arrived[2]))
    sources.append((0, latent, key_rope, doc_ids))
    masks = []
    for distance, key_latent, key_ropes, key_docs in sources:
        key_pos = (own_index - distance) * row_count + offsets
        allowed = (
            (key_docs[None, :] == doc_ids[:, None])
            & (key_pos[None, :] <= query_pos[:, None])
            & (key_pos[None, :] >= 0)
        )
        masks.append((allowed, jnp.any(allowed)))

    def score_tile(key_latent, key_ropes, allowed):
        product = jnp.einsum(
            "thl,sl->ths", query_latent, key_latent, preferred_element_type=jnp.float32
        ) + jnp.einsum("thr,sr->ths", rope_heads, key_ropes, preferred_element_type=jnp.float32)
        return jnp.where(allowed[:, None, :], score_scale * product, negative)

    scores = [
        score_tile(source[1], source[2], allowed)
        for source, (allowed, needed) in zip(sources, masks)
    ]
    row_max = reduce(jnp.maximum, [jnp.max(tile, axis=2, keepdims=True) for tile in scores])
    weights = [
        jnp.where(allowed[:, None, :], jnp.exp(tile - row_max), 0.0)
        for tile, (allowed, needed) in zip(scores, masks)
    ]
    denominator = reduce(jnp.add, [jnp.sum(tile, axis=2, keepdims=True) for tile in weights])
    probability = [tile / denominator for tile in weights]
    prob_low = [tile.astype(jnp.bfloat16) for tile in probability]

    def value_tile(low_tile, key_latent):
        return jnp.einsum("ths,sl->thl", low_tile, key_latent, preferred_element_type=jnp.float32)

    summed = reduce(
        jnp.add, [value_tile(prob_low[index], sources[index][1]) for index in range(len(sources))]
    )
    attended = summed.astype(jnp.bfloat16)
    row_delta = jnp.sum(grad_out.astype(jnp.float32) * summed, axis=2, keepdims=True)

    def grad_tile(prob_tile, low_tile, key_latent, key_ropes):
        grad_prob = jnp.einsum(
            "thl,sl->ths", grad_out, key_latent, preferred_element_type=jnp.float32
        )
        grad_score = (score_scale * prob_tile * (grad_prob - row_delta)).astype(jnp.bfloat16)
        return (
            jnp.einsum("ths,sl->thl", grad_score, key_latent, preferred_element_type=jnp.float32),
            jnp.einsum("ths,sr->thr", grad_score, key_ropes, preferred_element_type=jnp.float32),
            jnp.einsum("ths,thl->sl", grad_score, query_latent, preferred_element_type=jnp.float32)
            + jnp.einsum("ths,thl->sl", low_tile, grad_out, preferred_element_type=jnp.float32),
            jnp.einsum("ths,thr->sr", grad_score, rope_heads, preferred_element_type=jnp.float32),
        )

    grads = [
        grad_tile(probability[index], prob_low[index], sources[index][1], sources[index][2])
        for index in range(len(sources))
    ]
    grad_query = reduce(jnp.add, [tile[0] for tile in grads]).astype(jnp.bfloat16)
    grad_query_rope = (
        reduce(jnp.add, [tile[1] for tile in grads])
        .reshape(row_count, head_count * rope_width)
        .astype(jnp.bfloat16)
    )
    total_latent = grads[-1][2]
    total_rope = grads[-1][3]
    for block_slot in range(len(sources) - 1):
        distance = sources[block_slot][0]
        back_latent, back_rope = from_behind(
            (grads[block_slot][2], grads[block_slot][3]), "ctx", -distance
        )
        total_latent = total_latent + back_latent
        total_rope = total_rope + back_rope
    grad_latent, grad_key_rope = lax.psum((total_latent, total_rope), "head")
    return (attended, grad_query, grad_query_rope, grad_latent, grad_key_rope)


def solution(mesh):
    in_specs = (
        P("ctx", "head", None),
        P("ctx", "head"),
        P("ctx", None),
        P("ctx", None),
        P("ctx"),
        P("ctx", "head", None),
    )
    out_specs = (
        P("ctx", "head", None),
        P("ctx", "head", None),
        P("ctx", "head"),
        P("ctx", None),
        P("ctx", None),
    )
    return jax.shard_map(
        per_device, mesh=mesh, in_specs=in_specs, out_specs=out_specs, check_vma=False
    )
```

profile of v0, /device:TPU:1, one launch (start us, length us, event | category | flops | bytes accessed | tf_op | source)
XLA Modules:
  0.0 384.0 jit_solution(9431196279911091875)
XLA Ops:
  7.2 4.4 %collective-permute-start = (s32[128]{0:T(128)}, s32[128]{0:T(128)S(1)}, u32[]{:S(2)}, u32[]{:S(2)}) collective-permute-start(s32[128]{0:T(128)} %param.10), channel_id=1, source_target_pairs={{0,64},{16,80},{32,96},{48,112},{64,128},{80,144},{96,160},{112,17... | collective-permute-start | bytes 1544 | tf_op jit(solution)/shard_map/ppermute | solution.py:15
  11.6 4.6 %collective-permute-start.3 = (s32[128]{0:T(128)}, s32[128]{0:T(128)S(1)}, u32[]{:S(2)}, u32[]{:S(2)}) collective-permute-start(s32[128]{0:T(128)} %param.10), channel_id=1, source_target_pairs={{0,48},{16,64},{32,80},{48,96},{64,112},{80,128},{96,144},{112,160... | collective-permute-start | bytes 1544 | tf_op jit(solution)/shard_map/ppermute | solution.py:15
  16.3 3.6 collective-permute-start.6
  19.9 2.6 collective-permute-start.9
  22.5 3.5 collective-permute-start.11
  26.1 1.0 copy.71
  27.1 1.0 fusion.93
  28.2 4.8 %collective-permute-start.8 = (bf16[128,64]{0,1:T(8,128)(2,1)}, bf16[128,64]{0,1:T(8,128)(2,1)S(1)}, u32[]{:S(2)}, u32[]{:S(2)}) collective-permute-start(bf16[128,64]{0,1:T(8,128)(2,1)} %param.9), channel_id=1, source_target_pairs={{0,32},{16,48},{32,64},{48,80},{64,96},{80,112},{96,128},{112,144}... | collective-permute-start | bytes 49160 | tf_op jit(solution)/shard_map/ppermute | solution.py:15
  33.0 2.0 collective-permute-start.10
  35.0 5.7 %collective-permute-start.7 = (bf16[128,512]{1,0:T(8,128)(2,1)}, bf16[128,512]{1,0:T(8,128)(2,1)S(1)}, u32[]{:S(2)}, u32[]{:S(2)}) collective-permute-start(bf16[128,512]{1,0:T(8,128)(2,1)} %param.8), channel_id=1, source_target_pairs={{0,32},{16,48},{32,64},{48,80},{64,96},{80,112},{96,128},{112,144}... | collective-permute-start | bytes 393224 | tf_op jit(solution)/shard_map/ppermute | solution.py:15
  40.8 3.5 collective-permute-start.2
  44.3 1.1 and_and_fusion.4
  45.4 2.1 fusion.140
  47.6 3.6 collective-permute-start.1
  51.4 4.0 %collective-permute-start.5 = (bf16[128,64]{0,1:T(8,128)(2,1)S(1)}, bf16[128,64]{0,1:T(8,128)(2,1)S(1)}, u32[]{:S(2)}, u32[]{:S(2)}) collective-permute-start(bf16[128,64]{0,1:T(8,128)(2,1)S(1)} %copy-done.8), channel_id=1, source_target_pairs={{0,48},{16,64},{32,80},{48,96},{64,112},{80,128},{96,144},{112,160... | collective-permute-start | bytes 49160 | tf_op jit(solution)/shard_map/ppermute | solution.py:15
  55.7 3.3 collective-permute-start.4
  59.6 0.8 fusion.141
  68.6 1.2 multiply_reduce_fusion
  69.9 0.8 fusion.15
  71.4 0.8 fusion.16
  72.2 0.8 convolution_bitcast_fusion.10
  73.0 1.5 collective-permute-start.19
  75.3 0.8 convolution_bitcast_fusion.12
  76.9 0.8 convolution_bitcast_fusion.13
  77.8 1.4 fusion.28
  79.2 1.3 collective-permute-start.12
  80.5 1.5 fusion.29
  82.0 1.3 collective-permute-start.13
  83.3 0.8 fusion.17
  84.1 1.4 fusion.30
  85.5 1.3 collective-permute-start.14
  86.8 1.4 fusion.31
  88.2 1.3 collective-permute-start.15
  91.4 0.9 fusion.32
  92.8 0.8 convolution_bitcast_fusion.11
  93.7 1.7 copy.119
  95.3 1.5 copy.118
  96.9 1.5 copy.117
  99.3 1.3 collective-permute-start.17
  100.6 1.3 collective-permute-start.16
  101.9 1.3 collective-permute-start.18
  103.2 2.6 fusion.27
  105.9 2.5 collective-permute-done.17
  108.3 3.1 collective-permute-done.16
  111.5 1.0 fusion.36
  112.4 118.0 %psum.15 = f32[128,64]{0,1:T(8,128)} all-reduce(f32[128,64]{0,1:T(8,128)S(1)} %fusion.36), channel_id=1, replica_groups=mesh['ctx'=32,'head'=16] {'head'}, use_global_device_ids=true, to_apply=%region_12.13 | all-reduce | flops 8192 | bytes 65536 | tf_op jit(solution)/shard_map/psum | solution.py:101
  230.4 145.1 %all-reduce.2.cloned.1.call-done = f32[128,512]{1,0:T(8,128)} async-done(((f32[128,512]{1,0:T(8,128)}), f32[128,512]{1,0:T(8,128)}) %all-reduce.2.cloned.1.call-update) | async-done | bytes 262160 | tf_op jit(solution)/shard_map/psum | solution.py:101
  375.5 1.7 copy.197
  (80 shorter events, 14.8 us)
Async XLA Ops:
  7.2 44.2 %copy-start.8 = (bf16[128,64]{0,1:T(8,128)(2,1)S(1)}, bf16[128,64]{0,1:T(8,128)(2,1)}, u32[]{:S(2)}) copy-start(bf16[128,64]{0,1:T(8,128)(2,1)} %param.9) | copy-start | bytes 49156
  7.2 40.4 %copy-start.5 = (bf16[128,512]{1,0:T(8,128)(2,1)S(1)}, bf16[128,512]{1,0:T(8,128)(2,1)}, u32[]{:S(2)}) copy-start(bf16[128,512]{1,0:T(8,128)(2,1)} %param.8) | copy-start | bytes 393220
  7.2 368.3 %all-reduce.2.cloned.1.call-start = ((), (), s32[]{:S(2)}) async-start(), calls=%async_computation | async-start | bytes 524288 | tf_op jit(solution)/shard_map/psum | solution.py:101
  7.2 20.9 %collective-permute-start = (s32[128]{0:T(128)}, s32[128]{0:T(128)S(1)}, u32[]{:S(2)}, u32[]{:S(2)}) collective-permute-start(s32[128]{0:T(128)} %param.10), channel_id=1, source_target_pairs={{0,64},{16,80},{32,96},{48,112},{64,128},{80,144},{96,160},{112,17... | collective-permute-start | bytes 1544 | tf_op jit(solution)/shard_map/ppermute | solution.py:15
  11.6 21.4 %collective-permute-start.3 = (s32[128]{0:T(128)}, s32[128]{0:T(128)S(1)}, u32[]{:S(2)}, u32[]{:S(2)}) collective-permute-start(s32[128]{0:T(128)} %param.10), channel_id=1, source_target_pairs={{0,48},{16,64},{32,80},{48,96},{64,112},{80,128},{96,144},{112,160... | collective-permute-start | bytes 1544 | tf_op jit(solution)/shard_map/ppermute | solution.py:15
  16.3 18.7 %collective-permute-start.6 = (s32[128]{0:T(128)}, s32[128]{0:T(128)S(1)}, u32[]{:S(2)}, u32[]{:S(2)}) collective-permute-start(s32[128]{0:T(128)} %param.10), channel_id=1, source_target_pairs={{0,32},{16,48},{32,64},{48,80},{64,96},{80,112},{96,128},{112,144}... | collective-permute-start | bytes 1544 | tf_op jit(solution)/shard_map/ppermute | solution.py:15
  19.9 20.9 %collective-permute-start.9 = (s32[128]{0:T(128)}, s32[128]{0:T(128)S(1)}, u32[]{:S(2)}, u32[]{:S(2)}) collective-permute-start(s32[128]{0:T(128)} %param.10), channel_id=1, source_target_pairs={{0,16},{16,32},{32,48},{48,64},{64,80},{80,96},{96,112},{112,128},... | collective-permute-start | bytes 1544 | tf_op jit(solution)/shard_map/ppermute | solution.py:15
  22.5 25.0 %collective-permute-start.11 = (bf16[128,64]{0,1:T(8,128)(2,1)}, bf16[128,64]{0,1:T(8,128)(2,1)S(1)}, u32[]{:S(2)}, u32[]{:S(2)}) collective-permute-start(bf16[128,64]{0,1:T(8,128)(2,1)} %param.9), channel_id=1, source_target_pairs={{0,16},{16,32},{32,48},{48,64},{64,80},{80,96},{96,112},{112,128},... | collective-permute-start | bytes 49160 | tf_op jit(solution)/shard_map/ppermute | solution.py:15
  28.2 23.2 %collective-permute-start.8 = (bf16[128,64]{0,1:T(8,128)(2,1)}, bf16[128,64]{0,1:T(8,128)(2,1)S(1)}, u32[]{:S(2)}, u32[]{:S(2)}) collective-permute-start(bf16[128,64]{0,1:T(8,128)(2,1)} %param.9), channel_id=1, source_target_pairs={{0,32},{16,48},{32,64},{48,80},{64,96},{80,112},{96,128},{112,144}... | collective-permute-start | bytes 49160 | tf_op jit(solution)/shard_map/ppermute | solution.py:15
  33.0 26.6 %collective-permute-start.10 = (bf16[128,512]{1,0:T(8,128)(2,1)}, bf16[128,512]{1,0:T(8,128)(2,1)S(1)}, u32[]{:S(2)}, u32[]{:S(2)}) collective-permute-start(bf16[128,512]{1,0:T(8,128)(2,1)} %param.8), channel_id=1, source_target_pairs={{0,16},{16,32},{32,48},{48,64},{64,80},{80,96},{96,112},{112,128},... | collective-permute-start | bytes 393224 | tf_op jit(solution)/shard_map/ppermute | solution.py:15
  35.0 25.4 %collective-permute-start.7 = (bf16[128,512]{1,0:T(8,128)(2,1)}, bf16[128,512]{1,0:T(8,128)(2,1)S(1)}, u32[]{:S(2)}, u32[]{:S(2)}) collective-permute-start(bf16[128,512]{1,0:T(8,128)(2,1)} %param.8), channel_id=1, source_target_pairs={{0,32},{16,48},{32,64},{48,80},{64,96},{80,112},{96,128},{112,144}... | collective-permute-start | bytes 393224 | tf_op jit(solution)/shard_map/ppermute | solution.py:15
  40.8 14.9 %collective-permute-start.2 = (bf16[128,64]{0,1:T(8,128)(2,1)}, bf16[128,64]{0,1:T(8,128)(2,1)S(1)}, u32[]{:S(2)}, u32[]{:S(2)}) collective-permute-start(bf16[128,64]{0,1:T(8,128)(2,1)} %param.9), channel_id=1, source_target_pairs={{0,64},{16,80},{32,96},{48,112},{64,128},{80,144},{96,160},{112,17... | collective-permute-start | bytes 49160 | tf_op jit(solution)/shard_map/ppermute | solution.py:15
  45.4 24.5 %copy-start.6 = (pred[128,128]{0,1:T(8,128)(4,1)}, pred[128,128]{0,1:T(8,128)(4,1)S(1)}, u32[]{:S(2)}) copy-start(pred[128,128]{0,1:T(8,128)(4,1)S(1)} %get-tuple-element.24) | copy-start | bytes 49156
  45.4 14.2 %copy-start = (bf16[128,8,512]{2,1,0:T(8,128)(2,1)S(1)}, bf16[128,8,512]{2,1,0:T(8,128)(2,1)}, u32[]{:S(2)}) copy-start(bf16[128,8,512]{2,1,0:T(8,128)(2,1)} %param.6) | copy-start | bytes 3145732
  47.5 22.4 %copy-start.1 = (f32[128,8,128]{0,2,1:T(8,128)}, f32[128,8,128]{0,2,1:T(8,128)S(1)}, u32[]{:S(2)}) copy-start(f32[128,8,128]{0,2,1:T(8,128)S(1)} %get-tuple-element.28) | copy-start | bytes 1572868
  47.6 13.7 %collective-permute-start.1 = (bf16[128,512]{1,0:T(8,128)(2,1)S(1)}, bf16[128,512]{1,0:T(8,128)(2,1)S(1)}, u32[]{:S(2)}, u32[]{:S(2)}) collective-permute-start(bf16[128,512]{1,0:T(8,128)(2,1)S(1)} %copy-done.5), channel_id=1, source_target_pairs={{0,64},{16,80},{32,96},{48,112},{64,128},{80,144},{96,160},{112,17... | collective-permute-start | bytes 393224 | tf_op jit(solution)/shard_map/ppermute | solution.py:15
  51.4 7.9 %collective-permute-start.5 = (bf16[128,64]{0,1:T(8,128)(2,1)S(1)}, bf16[128,64]{0,1:T(8,128)(2,1)S(1)}, u32[]{:S(2)}, u32[]{:S(2)}) collective-permute-start(bf16[128,64]{0,1:T(8,128)(2,1)S(1)} %copy-done.8), channel_id=1, source_target_pairs={{0,48},{16,64},{32,80},{48,96},{64,112},{80,128},{96,144},{112,160... | collective-permute-start | bytes 49160 | tf_op jit(solution)/shard_map/ppermute | solution.py:15
  55.7 6.3 %collective-permute-start.4 = (bf16[128,512]{1,0:T(8,128)(2,1)S(1)}, bf16[128,512]{1,0:T(8,128)(2,1)S(1)}, u32[]{:S(2)}, u32[]{:S(2)}) collective-permute-start(bf16[128,512]{1,0:T(8,128)(2,1)S(1)} %copy-done.5), channel_id=1, source_target_pairs={{0,48},{16,64},{32,80},{48,96},{64,112},{80,128},{96,144},{112,160... | collective-permute-start | bytes 393224 | tf_op jit(solution)/shard_map/ppermute | solution.py:15
  62.9 1.2 copy-start.3
  73.0 32.9 %collective-permute-start.19 = (f32[128,64]{0,1:T(8,128)}, f32[128,64]{0,1:T(8,128)}, u32[]{:S(2)}, u32[]{:S(2)}) collective-permute-start(f32[128,64]{0,1:T(8,128)} %convolution_bitcast_fusion.10), channel_id=1, source_target_pairs={{16,0},{32,16},{48,32},{64,48},{80,64},{96,80},{112,96},{128,112},... | collective-permute-start | bytes 98312 | tf_op jit(solution)/shard_map/ppermute | solution.py:15
  79.2 20.0 %collective-permute-start.12 = (f32[128,512]{1,0:T(8,128)}, f32[128,512]{1,0:T(8,128)}, u32[]{:S(2)}, u32[]{:S(2)}) collective-permute-start(f32[128,512]{1,0:T(8,128)} %fusion.28), channel_id=1, source_target_pairs={{64,0},{80,16},{96,32},{112,48},{128,64},{144,80},{160,96},{176,11... | collective-permute-start | bytes 786440 | tf_op jit(solution)/shard_map/ppermute | solution.py:15
  82.0 18.6 %collective-permute-start.13 = (f32[128,512]{1,0:T(8,128)}, f32[128,512]{1,0:T(8,128)}, u32[]{:S(2)}, u32[]{:S(2)}) collective-permute-start(f32[128,512]{1,0:T(8,128)} %fusion.29), channel_id=1, source_target_pairs={{48,0},{64,16},{80,32},{96,48},{112,64},{128,80},{144,96},{160,112... | collective-permute-start | bytes 786440 | tf_op jit(solution)/shard_map/ppermute | solution.py:15
  85.5 16.4 %collective-permute-start.14 = (f32[128,512]{1,0:T(8,128)}, f32[128,512]{1,0:T(8,128)}, u32[]{:S(2)}, u32[]{:S(2)}) collective-permute-start(f32[128,512]{1,0:T(8,128)} %fusion.30), channel_id=1, source_target_pairs={{32,0},{48,16},{64,32},{80,48},{96,64},{112,80},{128,96},{144,112}... | collective-permute-start | bytes 786440 | tf_op jit(solution)/shard_map/ppermute | solution.py:15
  88.2 15.0 %collective-permute-start.15 = (f32[128,512]{1,0:T(8,128)}, f32[128,512]{1,0:T(8,128)}, u32[]{:S(2)}, u32[]{:S(2)}) collective-permute-start(f32[128,512]{1,0:T(8,128)} %fusion.31), channel_id=1, source_target_pairs={{16,0},{32,16},{48,32},{64,48},{80,64},{96,80},{112,96},{128,112},... | collective-permute-start | bytes 786440 | tf_op jit(solution)/shard_map/ppermute | solution.py:15
  95.3 3.1 copy-start.2
  95.3 3.1 copy-start.4
  95.3 3.1 copy-start.7
  98.4 0.8 copy-start.9
  98.4 2.1 copy-start.10
  98.5 3.4 copy-start.11
  99.3 9.1 %collective-permute-start.17 = (f32[128,64]{0,1:T(8,128)S(1)}, f32[128,64]{0,1:T(8,128)S(1)}, u32[]{:S(2)}, u32[]{:S(2)}) collective-permute-start(f32[128,64]{0,1:T(8,128)S(1)} %copy-done.9), channel_id=1, source_target_pairs={{48,0},{64,16},{80,32},{96,48},{112,64},{128,80},{144,96},{160,112... | collective-permute-start | bytes 98312 | tf_op jit(solution)/shard_map/ppermute | solution.py:15
  100.6 10.9 %collective-permute-start.16 = (f32[128,64]{0,1:T(8,128)S(1)}, f32[128,64]{0,1:T(8,128)S(1)}, u32[]{:S(2)}, u32[]{:S(2)}) collective-permute-start(f32[128,64]{0,1:T(8,128)S(1)} %copy-done.10), channel_id=1, source_target_pairs={{64,0},{80,16},{96,32},{112,48},{128,64},{144,80},{160,96},{176,11... | collective-permute-start | bytes 98312 | tf_op jit(solution)/shard_map/ppermute | solution.py:15
  101.9 9.6 %collective-permute-start.18 = (f32[128,64]{0,1:T(8,128)S(1)}, f32[128,64]{0,1:T(8,128)S(1)}, u32[]{:S(2)}, u32[]{:S(2)}) collective-permute-start(f32[128,64]{0,1:T(8,128)S(1)} %copy-done.11), channel_id=1, source_target_pairs={{32,0},{48,16},{64,32},{80,48},{96,64},{112,80},{128,96},{144,112}... | collective-permute-start | bytes 98312 | tf_op jit(solution)/shard_map/ppermute | solution.py:15
Sparse Core Ops, SparseCore 0:
  106.0 269.4 all-reduce.1
where the time goes:
time: 385 us; the launch traced here: 384 us
  waiting for transfers between devices  151 us (39%)
  blocking collectives  118 us (31%)
  starting transfers between devices  56.3 us (15%)
  matrix products  34.9 us (9%)
  between operations  14.8 us (4%)
  local copies, waits for them, and re-layouts  7.7 us (2%)
    psum x1, waiting for transfers between devices, per_device(): grad_latent, grad_key_rope = lax.psum((total_latent, total_rope), 'head')  145 us
    psum x1, blocking collectives, per_device(): grad_latent, grad_key_rope = lax.psum((total_latent, total_rope), 'head')  118 us
    ppermute x20, starting transfers between devices, from_behind(): return lax.ppermute(x, axis, pairs)  56.3 us
    dot_general x5, matrix products, grad_tile(): jnp.einsum('ths,thl->sl', grad_score, query_latent, preferred_element_typ...  8.43 us
  transfers between devices with their start and end apart: 21, of which 3 were waited for; matrix products, arithmetic and copies ran while one was open for 8% of the time, Pallas kernels for 0%

commit v1 on v0

v1 whole, which is shorter than its diff:
```python
import functools

import jax
import jax.numpy as jnp
from jax import lax
from jax.experimental import pallas as pl
from jax.experimental.pallas import tpu as pltpu
from jax.sharding import PartitionSpec as P

SCORE_SCALE = 192.0 ** (-0.5)
LOG2E = 1.4426950408889634
NEGATIVE = -1e30
MESH = pl.DeviceIdType.MESH

TOK = 128
HEADS = 8
ROWS = TOK * HEADS
LAT = 512
ROPE = 64
EXT = 640
BLOCKS = 5
KEYS = TOK * BLOCKS
HALF = EXT // 2
PIECE = HALF // 4
NT = (((1,), (1,)), ((), ()))
NN = (((1,), (0,)), ((), ()))
TILE = 256
CHUNK = 64


def dot(a, b, dims=NN):
    return lax.dot_general(a, b, dims, preferred_element_type=jnp.float32)


def iota(shape, dim):
    return lax.broadcasted_iota(jnp.int32, shape, dim)


def kernel(
    ql, qr, lat, kr, doc, go,
    att, dq, dqr, gl, gk,
    qx, g, qxt, gt, kx, s_all, gp_all, docq, p_all, gs_all,
    qr_v, lat_v, kr_v, doc_v, o_v, dq_v, dqr_v, gl_v, gk_v,
    part, part_in, summed, pieces_in, b_out, b_in, a_out, a_in, total,
    in_sem, out_sem, hz_s, hz_r, hy_s, hy_r, hc_s, hc_r,
    cs_s, cs_r, xy_s, xy_r, zb_s, zb_r, zh_s, zh_r, ag_s, ag_r,
):
    ctx = lax.axis_index("ctx")
    head = lax.axis_index("head")
    z = lax.rem(head // 8 * 8 + ctx // 4, 16)
    y = lax.rem(ctx, 4)
    x = lax.rem(head // 2, 4)
    c = lax.rem(head, 2)

    def device(dz=0, dy=0, dx=0, dc=0):
        zz = lax.rem(z + dz, 16)
        yy = lax.rem(y + dy, 4)
        xx = lax.rem(x + dx, 4)
        cc = lax.rem(c + dc, 2)
        return (lax.rem(zz, 8) * 4 + yy, zz // 8 * 8 + xx * 2 + cc)

    def remote(src, dst, send, recv, to):
        return pltpu.make_async_remote_copy(
            src_ref=src, dst_ref=dst, send_sem=send, recv_sem=recv,
            device_id=to, device_id_type=MESH,
        )

    partners = [dict(dy=dy, dx=dx) for dy in range(4) for dx in range(4) if dy or dx]
    partners += [dict(dx=dx, dc=1) for dx in range(4)]
    partners += [dict(dz=1), dict(dz=15), dict(dz=8)]
    barrier = pltpu.get_barrier_semaphore()
    for partner in partners:
        pl.semaphore_signal(barrier, inc=1, device_id=device(**partner), device_id_type=MESH)

    loads = [
        pltpu.make_async_copy(src, dst, in_sem.at[n])
        for n, (src, dst) in enumerate([
            (lat, lat_v), (kr, kr_v), (doc, doc_v), (qr, qr_v),
            (ql, qx.at[:, pl.ds(0, LAT)]), (go, g),
        ])
    ]
    for load in loads:
        load.start()

    for load in loads[:3]:
        load.wait()
    doc_row = jnp.broadcast_to(doc_v[...].astype(jnp.float32), (TOK, TOK))
    diagonal = iota((TOK, TOK), 0) == iota((TOK, TOK), 1)
    doc_col = jnp.sum(jnp.where(diagonal, doc_row, 0.0), axis=1, keepdims=True)
    kx[0:TOK, 0:LAT] = lat_v[...]
    kx[0:TOK, LAT:LAT + ROPE] = kr_v[...]
    kx[0:TOK, LAT + ROPE:EXT] = jnp.where(
        iota((TOK, ROPE), 1) == 0, doc_col, 0.0
    ).astype(jnp.bfloat16)

    pl.semaphore_wait(barrier, len(partners))

    half_rows = TOK // 2

    def half(d):
        return kx.at[pl.ds(pl.multiple_of(d * TOK + c * half_rows, half_rows), half_rows)]

    hz = remote(half(0), half(4), hz_s, hz_r, device(dz=1))
    hz.start()

    def hy(j, src):
        return remote(half(src), half(j), hy_s.at[j - 1], hy_r.at[j - 1], device(dy=j))

    for j in (3, 2, 1):
        @pl.when(y + j < 4)
        def _():
            hy(j, 0).start()

    def hc(d):
        return remote(half(d), half(d), hc_s.at[d - 1], hc_r.at[d - 1], device(dc=1))

    hz.wait_recv()
    for j in (2, 1, 3):
        @pl.when(y + j >= 4)
        def _():
            hy(j, 4).start()
    hc(4).start()

    docq[...] = dot(
        (iota((ROWS, TOK), 0) // HEADS == iota((ROWS, TOK), 1)).astype(jnp.bfloat16),
        jnp.broadcast_to(doc_col, (TOK, TOK)).astype(jnp.bfloat16),
    )
    loads[3].wait()
    lanes = iota((TILE, LAT), 1) // ROPE
    heads = lax.rem(iota((TILE, LAT), 0), HEADS)
    own_head = lanes == heads
    for r in range(0, ROWS, TILE):
        spread = (r // HEADS + iota((TILE, TOK), 0) // HEADS == iota((TILE, TOK), 1)).astype(jnp.bfloat16)
        wide = jnp.where(own_head, dot(spread, qr_v[...]), 0.0)
        pair = (wide[:, 0:128] + wide[:, 128:256]) + (wide[:, 256:384] + wide[:, 384:512])
        low = jnp.where(iota((TILE, 128), 1) < ROPE, pair + pltpu.roll(pair, ROPE, 1), 0.0)
        qx[r:r + TILE, LAT:EXT] = low.astype(jnp.bfloat16)
    loads[4].wait()
    loads[5].wait()
    for r in range(0, ROWS, TILE):
        s_all[r:r + TILE, 0:TOK] = dot(qx[r:r + TILE, :], kx[0:TOK, :], NT)
        gp_all[r:r + TILE, 0:TOK] = dot(g[r:r + TILE, :], kx[0:TOK, 0:LAT], NT)
    for r in range(0, ROWS, TILE):
        qxt[:, r:r + TILE] = qx[r:r + TILE, :].T
        gt[:, r:r + TILE] = g[r:r + TILE, :].T

    for j in (3, 1, 2):
        hy(j, 0).wait_recv()
        hc(j).start()
    for d in (4, 3, 1, 2):
        hc(d).wait_recv()

    pick = (iota((8, 128), 1) == ROPE).astype(jnp.bfloat16)
    docs = [dot(pick, kx[d * TOK:(d + 1) * TOK, LAT:EXT], NT)[0:1] for d in range(BLOCKS)]
    for r in range(0, ROWS, TILE):
        s_all[r:r + TILE, TOK:KEYS] = dot(qx[r:r + TILE, :], kx[TOK:KEYS, :], NT)
        gp_all[r:r + TILE, TOK:KEYS] = dot(g[r:r + TILE, :], kx[TOK:KEYS, 0:LAT], NT)
        for q in range(r, r + TILE, CHUNK):
            rows = slice(q, q + CHUNK)
            doc_here = docq[rows, :]
            causal = q // HEADS + iota((CHUNK, TOK), 0) // HEADS >= iota((CHUNK, TOK), 1)
            score = []
            for d in range(BLOCKS):
                allowed = doc_here == docs[d]
                if d == 0:
                    allowed = allowed & causal
                score.append(jnp.where(allowed, s_all[rows, d * TOK:(d + 1) * TOK], NEGATIVE))
            most = functools.reduce(jnp.maximum, score)
            most = jnp.max(most, axis=1, keepdims=True) * (SCORE_SCALE * LOG2E)
            weight = [jnp.exp2(tile * (SCORE_SCALE * LOG2E) - most) for tile in score]
            gp = [gp_all[rows, d * TOK:(d + 1) * TOK] for d in range(BLOCKS)]
            norm = jnp.sum(functools.reduce(jnp.add, weight), axis=1, keepdims=True)
            delta = functools.reduce(jnp.add, [w * t for w, t in zip(weight, gp)])
            delta = jnp.sum(delta, axis=1, keepdims=True)
            inverse = 1.0 / norm
            delta = delta * inverse
            for d in range(BLOCKS):
                prob = weight[d] * inverse
                p_all[rows, d * TOK:(d + 1) * TOK] = prob.astype(jnp.bfloat16)
                gs_all[rows, d * TOK:(d + 1) * TOK] = (
                    (SCORE_SCALE * prob) * (gp[d] - delta)
                ).astype(jnp.bfloat16)

    own_half = pl.ds(pl.multiple_of(c * HALF, HALF), HALF)
    other_half = pl.ds(pl.multiple_of((1 - c) * HALF, HALF), HALF)

    def core_sum(d):
        return remote(
            part.at[d, other_half], part_in.at[d], cs_s.at[d], cs_r.at[d], device(dc=1)
        )

    def xy(d, i):
        to = device(dx=i) if d in (0, 4) else device(dx=i, dy=4 - d)
        here = pl.ds(pl.multiple_of(lax.rem(x + i, 4) * PIECE, PIECE), PIECE)
        return remote(
            summed.at[d, here], pieces_in.at[d, i], xy_s.at[d, i], xy_r.at[d, i], to
        )

    def remote_pieces(d):
        return [i for i in (2, 1, 3, 0) if d not in (0, 4) or i]

    def pass_on(d):
        core_sum(d).wait_recv()
        summed[d] = (
            part[d, own_half].astype(jnp.float32) + part_in[d].astype(jnp.float32)
        ).astype(jnp.bfloat16)
        for i in remote_pieces(d):
            xy(d, i).start()

    groups = [(1, 2), (3, 4), (0,)]
    for n, group in enumerate(groups):
        cols = slice(group[0] * TOK, (group[-1] + 1) * TOK)
        for f in range(0, EXT, 128):
            grads = dot(qxt[f:f + 128, :], gs_all[:, cols])
            if f < LAT:
                grads = grads + dot(gt[f:f + 128, :], p_all[:, cols])
            for k, d in enumerate(group):
                part[d, f:f + 128, :] = grads[:, k * TOK:(k + 1) * TOK].astype(jnp.bfloat16)
        for d in group:
            core_sum(d).start()
        if n:
            for d in groups[n - 1]:
                pass_on(d)

    def stores():
        return [
            pltpu.make_async_copy(src, dst, out_sem.at[n])
            for n, (src, dst) in enumerate([
                (o_v, att), (dq_v, dq), (dqr_v, dqr), (gl_v, gl), (gk_v, gk),
            ])
        ]

    def outputs(r):
        o_v[r:r + TILE, :] = dot(p_all[r:r + TILE, :], kx[:, 0:LAT]).astype(jnp.bfloat16)
        grads = dot(gs_all[r:r + TILE, :], kx[...])
        dq_v[r:r + TILE, :] = grads[:, 0:LAT].astype(jnp.bfloat16)
        low = jnp.where(iota((TILE, 128), 1) < ROPE, grads[:, LAT:EXT], 0.0)
        pair = low + pltpu.roll(low, ROPE, 1)
        wide = jnp.where(own_head, jnp.concatenate([pair] * 4, axis=1), 0.0).astype(jnp.bfloat16)
        tokens = TILE // HEADS
        gather = (iota((tokens, TILE), 1) // HEADS == iota((tokens, TILE), 0)).astype(jnp.bfloat16)
        dqr_v[r // HEADS:r // HEADS + tokens, :] = dot(gather, wide).astype(jnp.bfloat16)

    outputs(0)
    for d in groups[-1]:
        pass_on(d)
    for r in range(TILE, ROWS, TILE):
        outputs(r)
    for store in stores()[:3]:
        store.start()

    own_piece = pl.ds(pl.multiple_of(x * PIECE, PIECE), PIECE)

    def gathered(d):
        terms = [] if d in range(1, 4) else [summed[d, own_piece].astype(jnp.float32)]
        for i in remote_pieces(d):
            xy(d, i).wait_recv()
            terms.append(pieces_in[d, i].astype(jnp.float32))
        return functools.reduce(jnp.add, terms)

    b = jnp.zeros((PIECE, TOK), jnp.float32)
    a = jnp.zeros((PIECE, TOK), jnp.float32)
    for d in (1, 2, 3):
        term = gathered(d)
        same = y + d < 4
        a = a + jnp.where(same, term, 0.0)
        b = b + jnp.where(same, 0.0, term)
    b = b + gathered(4)
    b_out[...] = b.astype(jnp.bfloat16)
    zb = remote(b_out, b_in, zb_s, zb_r, device(dz=15))
    zb.start()
    a = a + gathered(0)
    zb.wait_recv()
    a = a + b_in[...].astype(jnp.float32)
    a_out[...] = a.astype(jnp.bfloat16)
    zh = remote(a_out, a_in, zh_s, zh_r, device(dz=8))
    zh.start()
    zh.wait_recv()
    mine = pl.ds(pl.multiple_of(c * HALF + x * PIECE, PIECE), PIECE)
    total[mine, :] = (
        a_out[...].astype(jnp.float32) + a_in[...].astype(jnp.float32)
    ).astype(jnp.bfloat16)
    spread_to = [(i, cc) for i in (2, 1, 3, 0) for cc in (0, 1) if i or cc]

    def ag(i, cc):
        return remote(
            total.at[mine], total.at[mine], ag_s.at[i, cc], ag_r.at[i, cc], device(dx=i, dc=cc)
        )

    for i, cc in spread_to:
        ag(i, cc).start()
    for i, cc in spread_to:
        ag(i, cc).wait_recv()
    turned = dot(diagonal.astype(jnp.bfloat16), total[...], NT)
    gl_v[...] = turned[:, 0:LAT]
    gk_v[...] = turned[:, LAT:LAT + ROPE]
    for store in stores()[3:]:
        store.start()

    hz.wait_send()
    for j in (1, 2, 3):
        hy(j, 0).wait_send()
    for d in (1, 2, 3, 4):
        hc(d).wait_send()
    for d in range(BLOCKS):
        core_sum(d).wait_send()
        for i in remote_pieces(d):
            xy(d, i).wait_send()
    zb.wait_send()
    zh.wait_send()
    for i, cc in spread_to:
        ag(i, cc).wait_send()
    for store in stores():
        store.wait()


def per_device(query_latent, query_rope, latent, key_rope, doc_ids, grad_out):
    bf16, f32 = jnp.bfloat16, jnp.float32
    dma = pltpu.SemaphoreType.DMA
    anywhere = pl.BlockSpec(memory_space=pl.ANY)
    attended, grad_query, grad_query_rope, grad_latent, grad_key_rope = pl.pallas_call(
        kernel,
        out_shape=(
            jax.ShapeDtypeStruct((ROWS, LAT), bf16),
            jax.ShapeDtypeStruct((ROWS, LAT), bf16),
            jax.ShapeDtypeStruct((TOK, LAT), bf16),
            jax.ShapeDtypeStruct((TOK, LAT), f32),
            jax.ShapeDtypeStruct((TOK, ROPE), f32),
        ),
        in_specs=[anywhere] * 6,
        out_specs=[anywhere] * 5,
        scratch_shapes=[
            pltpu.VMEM((ROWS, EXT), bf16),
            pltpu.VMEM((ROWS, LAT), bf16),
            pltpu.VMEM((EXT, ROWS), bf16),
            pltpu.VMEM((LAT, ROWS), bf16),
            pltpu.VMEM((KEYS, EXT), bf16),
            pltpu.VMEM((ROWS, KEYS), f32),
            pltpu.VMEM((ROWS, KEYS), f32),
            pltpu.VMEM((ROWS, TOK), f32),
            pltpu.VMEM((ROWS, KEYS), bf16),
            pltpu.VMEM((ROWS, KEYS), bf16),
            pltpu.VMEM((TOK, LAT), bf16),
            pltpu.VMEM((TOK, LAT), bf16),
            pltpu.VMEM((TOK, ROPE), bf16),
            pltpu.VMEM((1, TOK), jnp.int32),
            pltpu.VMEM((ROWS, LAT), bf16),
            pltpu.VMEM((ROWS, LAT), bf16),
            pltpu.VMEM((TOK, LAT), bf16),
            pltpu.VMEM((TOK, LAT), f32),
            pltpu.VMEM((TOK, ROPE), f32),
            pltpu.VMEM((BLOCKS, EXT, TOK), bf16),
            pltpu.VMEM((BLOCKS, HALF, TOK), bf16),
            pltpu.VMEM((BLOCKS, HALF, TOK), bf16),
            pltpu.VMEM((BLOCKS, 4, PIECE, TOK), bf16),
            pltpu.VMEM((PIECE, TOK), bf16),
            pltpu.VMEM((PIECE, TOK), bf16),
            pltpu.VMEM((PIECE, TOK), bf16),
            pltpu.VMEM((PIECE, TOK), bf16),
            pltpu.VMEM((EXT, TOK), bf16),
            dma((6,)), dma((5,)),
            dma, dma, dma((3,)), dma((3,)), dma((4,)), dma((4,)),
            dma((BLOCKS,)), dma((BLOCKS,)), dma((BLOCKS, 4)), dma((BLOCKS, 4)),
            dma, dma, dma, dma, dma((4, 2)), dma((4, 2)),
        ],
        compiler_params=pltpu.CompilerParams(
            collective_id=0, has_side_effects=True, vmem_limit_bytes=48 * 1024 * 1024
        ),
        cost_estimate=pl.CostEstimate(
            flops=9 * 2 * ROWS * KEYS * LAT // 2, bytes_accessed=5 * 1024 * 1024,
            transcendentals=ROWS * KEYS,
        ),
    )(
        query_latent.reshape(ROWS, LAT),
        query_rope,
        latent,
        key_rope,
        doc_ids.reshape(1, TOK),
        grad_out.reshape(ROWS, LAT),
    )
    return (
        attended.reshape(TOK, HEADS, LAT),
        grad_query.reshape(TOK, HEADS, LAT),
        grad_query_rope,
        grad_latent,
        grad_key_rope,
    )


def solution(mesh):
    in_specs = (
        P("ctx", "head", None),
        P("ctx", "head"),
        P("ctx", None),
        P("ctx", None),
        P("ctx"),
        P("ctx", "head", None),
    )
    out_specs = (
        P("ctx", "head", None),
        P("ctx", "head", None),
        P("ctx", "head"),
        P("ctx", None),
        P("ctx", None),
    )
    return jax.shard_map(
        per_device, mesh=mesh, in_specs=in_specs, out_specs=out_specs, check_vma=False
    )
```

time: 385 us -> 61.1 us (0.16)
  waiting for transfers between devices: 151 us -> 0 us
  blocking collectives: 118 us -> 0 us
  starting transfers between devices: 56.3 us -> 0 us
  Pallas kernels: 0 us -> 51.1 us
  matrix products: 34.9 us -> 0 us
  between operations: 14.8 us -> 0.67 us
    psum x1 -> x0, waiting for transfers between devices: 145 us -> none  [per_device(): grad_latent, grad_key_rope = lax.psum((total_latent, total_rope), 'head')]
    psum x1 -> x0, blocking collectives: 118 us -> none  [per_device(): grad_latent, grad_key_rope = lax.psum((total_latent, total_rope), 'head')]
    ppermute x20 -> x0, starting transfers between devices: 56.3 us -> none  [from_behind(): return lax.ppermute(x, axis, pairs)]
    pallas_call x0 -> x1, Pallas kernels: none -> 51.1 us  [per_device(): pl.pallas_call(kernel, out_shape=(jax.ShapeDtypeStruct((ROWS, LAT), bf16)...]
    dot_general x45 -> x0, matrix products: 34.9 us -> none  [the longest x5 8.43 us: grad_tile(): jnp.einsum('ths,thl->sl', grad_score, query_latent, preferred_element_typ...]
    ppermute x20 -> x0, waiting for transfers between devices: 5.62 us -> none  [from_behind(): return lax.ppermute(x, axis, pairs)]
    unnamed x29 -> x16, local copies, waits for them, and re-layouts: 7.7 us -> 9.08 us
  transfers between devices with their start and end apart: 21 -> 0, of which waited for: 3 -> 0; matrix products, arithmetic and copies ran while one was open for 8% -> 0% of each run, Pallas kernels for 0% -> 0%
where the time goes in v1:
time: 61.1 us; the launch traced here: 60.9 us
  Pallas kernels  51.1 us (84%)
  local copies, waits for them, and re-layouts  9.08 us (15%)
  between operations  0.67 us (1%)
    pallas_call x1, Pallas kernels, per_device(): pl.pallas_call(kernel, out_shape=(jax.ShapeDtypeStruct((ROWS, LAT), bf16)...  51.1 us
    unnamed x16, local copies, waits for them, and re-layouts  9.08 us

profile of v1, /device:TPU:1, one launch (start us, length us, event | category | flops | bytes accessed | tf_op | source)
XLA Modules:
  0.0 60.9 jit_solution(627058382883474410)
XLA Ops:
  0.6 0.0 copy-start.4
  0.6 0.8 %copy.11.kr = bf16[128,64]{1,0:T(8,128)(2,1)S(1)} copy(bf16[128,64]{0,1:T(8,128)(2,1)} %param.9) | data formatting | bytes 32768 | tf_op args[3]
  1.5 0.0 copy-done.4
  1.5 0.0 copy-start
  1.5 1.2 %copy-done = bf16[128,8,512]{2,1,0:T(8,128)(2,1)S(1)} copy-done((bf16[128,8,512]{2,1,0:T(8,128)(2,1)S(1)}, bf16[128,8,512]{2,1,0:T(8,128)(2,1)}, u32[]{:S(2)}) %copy-start) | copy-done | bytes 1048600
  2.7 0.0 copy-start.1
  2.7 1.2 %copy-done.1 = bf16[128,8,512]{2,1,0:T(8,128)(2,1)S(1)} copy-done((bf16[128,8,512]{2,1,0:T(8,128)(2,1)S(1)}, bf16[128,8,512]{2,1,0:T(8,128)(2,1)}, u32[]{:S(2)}) %copy-start.1) | copy-done | bytes 1048600
  3.9 0.0 copy-start.2
  3.9 0.9 %copy-done.2 = bf16[128,512]{1,0:T(8,128)(2,1)S(1)} copy-done((bf16[128,512]{1,0:T(8,128)(2,1)S(1)}, bf16[128,512]{1,0:T(8,128)(2,1)}, u32[]{:S(2)}) %copy-start.2) | copy-done | bytes 131096
  4.8 0.0 copy-start.3
  4.8 0.9 %copy-done.3 = bf16[128,512]{1,0:T(8,128)(2,1)S(1)} copy-done((bf16[128,512]{1,0:T(8,128)(2,1)S(1)}, bf16[128,512]{1,0:T(8,128)(2,1)}, u32[]{:S(2)}) %copy-start.3) | copy-done | bytes 131096
  5.7 51.1 %shard_map.101 = (bf16[1024,512]{1,0:T(8,128)(2,1)S(1)}, bf16[1024,512]{1,0:T(8,128)(2,1)S(1)}, bf16[128,512]{1,0:T(8,128)(2,1)S(1)}, f32[128,512]{1,0:T(8,128)S(1)}, f32[128,64]{1,0:T(8,128)S(1)}) custom-call(bf16[1024,512]{1,0:T(8,128)(2,1)S(1)} %bitcast.7, bf16[128,512]{1,0:T(8,128)(2,1)S(1)} %copy-done.2, bf16[128,512]{1,0:T(8,128)(2,1)S(1)} %copy-done.3, ...), custom_call_target="tpu_custom_call" | custom-call | flops 3019898880 | bytes 5242880 | tf_op jit(solution)/shard_map/pallas_call | solution.py:321
  56.9 0.7 %copy.12 = f32[128,64]{0,1:T(8,128)} copy(f32[128,64]{1,0:T(8,128)S(1)} %get-tuple-element.19) | data formatting | bytes 65536
  57.6 1.0 %copy.17 = bf16[128,8,512]{2,1,0:T(8,128)(2,1)} copy(bf16[128,8,512]{2,1,0:T(8,128)(2,1)S(1)} %bitcast.6) | data formatting | bytes 2097152
  58.5 1.0 %copy.18 = bf16[128,8,512]{2,1,0:T(8,128)(2,1)} copy(bf16[128,8,512]{2,1,0:T(8,128)(2,1)S(1)} %bitcast.5) | data formatting | bytes 2097152
  59.5 0.7 %copy.19 = bf16[128,512]{1,0:T(8,128)(2,1)} copy(bf16[128,512]{1,0:T(8,128)(2,1)S(1)} %get-tuple-element.27) | data formatting | bytes 262144
  60.2 0.7 %copy.20 = f32[128,512]{1,0:T(8,128)} copy(f32[128,512]{1,0:T(8,128)S(1)} %get-tuple-element.28) | data formatting | bytes 524288
Async XLA Ops:
  0.6 0.8 %copy-start.4 = (s32[128]{0:T(128)S(1)}, s32[128]{0:T(128)}, u32[]{:S(2)}) copy-start(s32[128]{0:T(128)} %param.10) | copy-start | bytes 1540
  1.5 1.2 %copy-start = (bf16[128,8,512]{2,1,0:T(8,128)(2,1)S(1)}, bf16[128,8,512]{2,1,0:T(8,128)(2,1)}, u32[]{:S(2)}) copy-start(bf16[128,8,512]{2,1,0:T(8,128)(2,1)} %param.6) | copy-start | bytes 3145732
  2.7 1.2 %copy-start.1 = (bf16[128,8,512]{2,1,0:T(8,128)(2,1)S(1)}, bf16[128,8,512]{2,1,0:T(8,128)(2,1)}, u32[]{:S(2)}) copy-start(bf16[128,8,512]{2,1,0:T(8,128)(2,1)} %param.11) | copy-start | bytes 3145732
  3.9 0.9 %copy-start.2 = (bf16[128,512]{1,0:T(8,128)(2,1)S(1)}, bf16[128,512]{1,0:T(8,128)(2,1)}, u32[]{:S(2)}) copy-start(bf16[128,512]{1,0:T(8,128)(2,1)} %qr.1) | copy-start | bytes 393220
  4.8 0.9 %copy-start.3 = (bf16[128,512]{1,0:T(8,128)(2,1)S(1)}, bf16[128,512]{1,0:T(8,128)(2,1)}, u32[]{:S(2)}) copy-start(bf16[128,512]{1,0:T(8,128)(2,1)} %lat.1) | copy-start | bytes 393220

commit v2 on v1

v2 whole, which is shorter than its diff:
```python
import functools

import jax
import jax.numpy as jnp
from jax import lax
from jax.experimental import pallas as pl
from jax.experimental.pallas import tpu as pltpu
from jax.sharding import PartitionSpec as P

SCORE_SCALE = 192.0 ** (-0.5)
LOG2E = 1.4426950408889634
NEGATIVE = -1e30
MESH = pl.DeviceIdType.MESH

TOK = 128
HEADS = 8
ROWS = TOK * HEADS
LAT = 512
ROPE = 64
EXT = 640
BLOCKS = 5
KEYS = TOK * BLOCKS
HALF = EXT // 2
PIECE = HALF // 4
NT = (((1,), (1,)), ((), ()))
NN = (((1,), (0,)), ((), ()))
TILE = 256
CHUNK = 64


def dot(a, b, dims=NN):
    return lax.dot_general(a, b, dims, preferred_element_type=jnp.float32)


def iota(shape, dim):
    return lax.broadcasted_iota(jnp.int32, shape, dim)


def products(qx, g, kx, s_all, gp_all, keys):
    for r in range(0, ROWS, TILE):
        s_all[r:r + TILE, keys] = dot(qx[r:r + TILE, :], kx[keys, :], NT)
        gp_all[r:r + TILE, keys] = dot(g[r:r + TILE, :], kx[keys, 0:LAT], NT)


def prepare(qx, g, qxt, gt, kx, s_all, gp_all, docq, qr_v, doc_col, own_head, loads):
    docq[...] = dot(
        (iota((ROWS, TOK), 0) // HEADS == iota((ROWS, TOK), 1)).astype(jnp.bfloat16),
        jnp.broadcast_to(doc_col, (TOK, TOK)).astype(jnp.bfloat16),
    )
    loads[3].wait()
    for r in range(0, ROWS, TILE):
        spread = (r // HEADS + iota((TILE, TOK), 0) // HEADS == iota((TILE, TOK), 1)).astype(jnp.bfloat16)
        wide = jnp.where(own_head, dot(spread, qr_v[...]), 0.0)
        pair = (wide[:, 0:128] + wide[:, 128:256]) + (wide[:, 256:384] + wide[:, 384:512])
        low = jnp.where(iota((TILE, 128), 1) < ROPE, pair + pltpu.roll(pair, ROPE, 1), 0.0)
        qx[r:r + TILE, LAT:EXT] = low.astype(jnp.bfloat16)
    loads[4].wait()
    loads[5].wait()
    products(qx, g, kx, s_all, gp_all, slice(0, TOK))
    for r in range(0, ROWS, TILE):
        qxt[:, r:r + TILE] = qx[r:r + TILE, :].T
        gt[:, r:r + TILE] = g[r:r + TILE, :].T


def scores(kx, s_all, gp_all, docq, p_all, gs_all):
    pick = (iota((8, 128), 1) == ROPE).astype(jnp.bfloat16)
    docs = [dot(pick, kx[d * TOK:(d + 1) * TOK, LAT:EXT], NT)[0:1] for d in range(BLOCKS)]
    for r in range(0, ROWS, TILE):
        for q in range(r, r + TILE, CHUNK):
            rows = slice(q, q + CHUNK)
            doc_here = docq[rows, :]
            causal = q // HEADS + iota((CHUNK, TOK), 0) // HEADS >= iota((CHUNK, TOK), 1)
            score = []
            for d in range(BLOCKS):
                allowed = doc_here == docs[d]
                if d == 0:
                    allowed = allowed & causal
                score.append(jnp.where(allowed, s_all[rows, d * TOK:(d + 1) * TOK], NEGATIVE))
            most = functools.reduce(jnp.maximum, score)
            most = jnp.max(most, axis=1, keepdims=True) * (SCORE_SCALE * LOG2E)
            weight = [jnp.exp2(tile * (SCORE_SCALE * LOG2E) - most) for tile in score]
            gp = [gp_all[rows, d * TOK:(d + 1) * TOK] for d in range(BLOCKS)]
            norm = jnp.sum(functools.reduce(jnp.add, weight), axis=1, keepdims=True)
            delta = functools.reduce(jnp.add, [w * t for w, t in zip(weight, gp)])
            delta = jnp.sum(delta, axis=1, keepdims=True)
            inverse = 1.0 / norm
            delta = delta * inverse
            for d in range(BLOCKS):
                prob = weight[d] * inverse
                p_all[rows, d * TOK:(d + 1) * TOK] = prob.astype(jnp.bfloat16)
                gs_all[rows, d * TOK:(d + 1) * TOK] = (
                    (SCORE_SCALE * prob) * (gp[d] - delta)
                ).astype(jnp.bfloat16)


def key_grads(qxt, gt, gs_all, p_all, part, group):
    cols = slice(group[0] * TOK, (group[-1] + 1) * TOK)
    for f in range(0, EXT, 128):
        grads = dot(qxt[f:f + 128, :], gs_all[:, cols])
        if f < LAT:
            grads = grads + dot(gt[f:f + 128, :], p_all[:, cols])
        for k, d in enumerate(group):
            part[d, f:f + 128, :] = grads[:, k * TOK:(k + 1) * TOK].astype(jnp.bfloat16)


def outputs(p_all, gs_all, kx, own_head, o_v, dq_v, dqr_v, r):
    o_v[r:r + TILE, :] = dot(p_all[r:r + TILE, :], kx[:, 0:LAT]).astype(jnp.bfloat16)
    grads = dot(gs_all[r:r + TILE, :], kx[...])
    dq_v[r:r + TILE, :] = grads[:, 0:LAT].astype(jnp.bfloat16)
    low = jnp.where(iota((TILE, 128), 1) < ROPE, grads[:, LAT:EXT], 0.0)
    pair = low + pltpu.roll(low, ROPE, 1)
    wide = jnp.where(own_head, jnp.concatenate([pair] * 4, axis=1), 0.0).astype(jnp.bfloat16)
    tokens = TILE // HEADS
    gather = (iota((tokens, TILE), 1) // HEADS == iota((tokens, TILE), 0)).astype(jnp.bfloat16)
    dqr_v[r // HEADS:r // HEADS + tokens, :] = dot(gather, wide).astype(jnp.bfloat16)


def kernel(
    ql, qr, lat, kr, doc, go,
    o_v, dq_v, dqr_v, gl_v, gk_v,
    qx, g, qxt, gt, kx, s_all, gp_all, docq, p_all, gs_all,
    qr_v, kr_v, doc_v,
    part, part_in, summed, pieces_in, b_out, b_in, a_out, a_in, total,
    in_sem, hz_s, hz_r, hy_s, hy_r, hc_s, hc_r,
    cs_s, cs_r, xy_s, xy_r, zb_s, zb_r, zh_s, zh_r, ag_s, ag_r, met, met_2, met_4,
):
    ctx = lax.axis_index("ctx")
    head = lax.axis_index("head")
    z = lax.rem(head // 8 * 8 + ctx // 4, 16)
    y = lax.rem(ctx, 4)
    x = lax.rem(head // 2, 4)
    c = lax.rem(head, 2)

    def device(dz=0, dy=0, dx=0, dc=0):
        zz = lax.rem(z + dz, 16)
        yy = lax.rem(y + dy, 4)
        xx = lax.rem(x + dx, 4)
        cc = lax.rem(c + dc, 2)
        return (lax.rem(zz, 8) * 4 + yy, zz // 8 * 8 + xx * 2 + cc)

    def remote(src, dst, send, recv, to):
        return pltpu.make_async_remote_copy(
            src_ref=src, dst_ref=dst, send_sem=send, recv_sem=recv,
            device_id=to, device_id_type=MESH,
        )

    partners = [dict(dy=1), dict(dy=2), dict(dy=3), dict(dz=1), dict(dz=15), dict(dc=1)]
    partners += [dict(dx=1), dict(dx=2), dict(dx=3)]
    barrier = pltpu.get_barrier_semaphore()
    for partner in partners:
        pl.semaphore_signal(barrier, inc=1, device_id=device(**partner), device_id_type=MESH)

    loads = [
        pltpu.make_async_copy(src, dst, in_sem.at[n])
        for n, (src, dst) in enumerate([
            (lat, kx.at[pl.ds(0, TOK), pl.ds(0, LAT)]), (kr, kr_v), (doc, doc_v), (qr, qr_v),
            (ql, qx.at[:, pl.ds(0, LAT)]), (go, g),
        ])
    ]
    for load in loads:
        load.start()

    for load in loads[:3]:
        load.wait()
    doc_row = jnp.broadcast_to(doc_v[...].astype(jnp.float32), (TOK, TOK))
    diagonal = iota((TOK, TOK), 0) == iota((TOK, TOK), 1)
    doc_col = jnp.sum(jnp.where(diagonal, doc_row, 0.0), axis=1, keepdims=True)
    kx[0:TOK, LAT:LAT + ROPE] = dot(diagonal.astype(jnp.bfloat16), kr_v[...], NT).astype(jnp.bfloat16)
    kx[0:TOK, LAT + ROPE:EXT] = jnp.where(
        iota((TOK, ROPE), 1) == 0, doc_col, 0.0
    ).astype(jnp.bfloat16)

    pl.semaphore_wait(barrier, len(partners))

    def tell(sem, *others):
        for other in others:
            pl.semaphore_signal(sem, inc=1, device_id=device(**other), device_id_type=MESH)

    half_rows = TOK // 2

    def half(d):
        return kx.at[pl.ds(pl.multiple_of(d * TOK + c * half_rows, half_rows), half_rows)]

    hz = remote(half(0), half(4), hz_s, hz_r, device(dz=1))
    hz.start()

    def hy(j, src):
        return remote(half(src), half(j), hy_s.at[j - 1], hy_r.at[j - 1], device(dy=j))

    for j in (3, 2, 1):
        @pl.when(y + j < 4)
        def _():
            hy(j, 0).start()

    tell(met, dict(dy=1), dict(dy=2), dict(dy=3), dict(dz=1), dict(dz=15))

    def hc(d):
        return remote(half(d), half(d), hc_s.at[d - 1], hc_r.at[d - 1], device(dc=1))

    hz.wait_recv()
    for j in (2, 1, 3):
        @pl.when(y + j >= 4)
        def _():
            hy(j, 4).start()
    hc(4).start()

    own_head = iota((TILE, LAT), 1) // ROPE == lax.rem(iota((TILE, LAT), 0), HEADS)
    prepare(qx, g, qxt, gt, kx, s_all, gp_all, docq, qr_v, doc_col, own_head, loads)

    pl.semaphore_wait(met, 5)
    tell(met_2, dict(dz=2), dict(dz=14))
    for j in (3, 1, 2):
        hy(j, 0).wait_recv()
        hc(j).start()
    for pair in ((3, 4), (1, 2)):
        for d in pair:
            hc(d).wait_recv()
        products(qx, g, kx, s_all, gp_all, slice(pair[0] * TOK, (pair[1] + 1) * TOK))
    pl.semaphore_wait(met_2, 2)
    tell(met_4, dict(dz=4), dict(dz=12))
    scores(kx, s_all, gp_all, docq, p_all, gs_all)

    own_half = pl.ds(pl.multiple_of(c * HALF, HALF), HALF)
    other_half = pl.ds(pl.multiple_of((1 - c) * HALF, HALF), HALF)

    def core_sum(d):
        return remote(
            part.at[d, other_half], part_in.at[d], cs_s.at[d], cs_r.at[d], device(dc=1)
        )

    def xy(d, i):
        to = device(dx=i) if d in (0, 4) else device(dx=i, dy=4 - d)
        here = pl.ds(pl.multiple_of(lax.rem(x + i, 4) * PIECE, PIECE), PIECE)
        return remote(
            summed.at[d, here], pieces_in.at[d, i], xy_s.at[d, i], xy_r.at[d, i], to
        )

    def remote_pieces(d):
        return [i for i in (2, 1, 3, 0) if d not in (0, 4) or i]

    def pass_on(d):
        core_sum(d).wait_recv()
        summed[d] = (
            part[d, own_half].astype(jnp.float32) + part_in[d].astype(jnp.float32)
        ).astype(jnp.bfloat16)
        for i in remote_pieces(d):
            xy(d, i).start()

    groups = [(1, 2), (3, 4), (0,)]
    for n, group in enumerate(groups):
        key_grads(qxt, gt, gs_all, p_all, part, group)
        for d in group:
            core_sum(d).start()
        if n:
            for d in groups[n - 1]:
                pass_on(d)

    outputs(p_all, gs_all, kx, own_head, o_v, dq_v, dqr_v, 0)
    for d in groups[-1]:
        pass_on(d)
    for r in range(TILE, ROWS, TILE):
        outputs(p_all, gs_all, kx, own_head, o_v, dq_v, dqr_v, r)

    own_piece = pl.ds(pl.multiple_of(x * PIECE, PIECE), PIECE)

    def gathered(d):
        terms = [] if d in range(1, 4) else [summed[d, own_piece].astype(jnp.float32)]
        for i in remote_pieces(d):
            xy(d, i).wait_recv()
            terms.append(pieces_in[d, i].astype(jnp.float32))
        return functools.reduce(jnp.add, terms)

    b = jnp.zeros((PIECE, TOK), jnp.float32)
    a = jnp.zeros((PIECE, TOK), jnp.float32)
    for d in (1, 2, 3):
        term = gathered(d)
        same = y + d < 4
        a = a + jnp.where(same, term, 0.0)
        b = b + jnp.where(same, 0.0, term)
    b = b + gathered(4)
    b_out[...] = b.astype(jnp.bfloat16)
    pl.semaphore_wait(met_4, 2)
    far_b = remote(b_out, b_in.at[1], zb_s.at[1], zb_r.at[1], device(dz=7))
    near_b = remote(b_out, b_in.at[0], zb_s.at[0], zb_r.at[0], device(dz=15))
    far_a = remote(a_out, a_in, zh_s, zh_r, device(dz=8))
    far_b.start()
    a = a + gathered(0)
    a_out[...] = a.astype(jnp.bfloat16)
    far_a.start()
    near_b.start()

    for copy in (near_b, far_b, far_a):
        copy.wait_recv()
    mine = pl.ds(pl.multiple_of(c * HALF + x * PIECE, PIECE), PIECE)
    total[mine, :] = (
        (a_out[...].astype(jnp.float32) + a_in[...].astype(jnp.float32))
        + (b_in[0].astype(jnp.float32) + b_in[1].astype(jnp.float32))
    ).astype(jnp.bfloat16)

    def ag(i):
        return remote(total.at[mine], total.at[mine], ag_s.at[i], ag_r.at[i], device(dx=i))

    for i in (2, 1, 3):
        ag(i).start()
    for i in (2, 1, 3):
        ag(i).wait_recv()
    last = remote(total.at[own_half], total.at[own_half], ag_s.at[0], ag_r.at[0], device(dc=1))
    last.start()
    last.wait_recv()
    gl_v[...] = dot(diagonal.astype(jnp.bfloat16), total[0:LAT, :], NT)
    gk_v[...] = total[LAT:LAT + ROPE, :].astype(jnp.float32)

    hz.wait_send()
    for j in (1, 2, 3):
        hy(j, 0).wait_send()
    for d in (1, 2, 3, 4):
        hc(d).wait_send()
    for d in range(BLOCKS):
        core_sum(d).wait_send()
        for i in remote_pieces(d):
            xy(d, i).wait_send()
    for copy in (near_b, far_b, far_a, ag(1), ag(2), ag(3), last):
        copy.wait_send()


def store(*refs):
    sources, targets, sem = refs[:5], refs[5:10], refs[10]
    copies = [pltpu.make_async_copy(sources[n], targets[n], sem.at[n]) for n in range(5)]
    for copy in copies:
        copy.start()
    for copy in copies:
        copy.wait()


def per_device(query_latent, query_rope, latent, key_rope, doc_ids, grad_out):
    bf16, f32 = jnp.bfloat16, jnp.float32
    dma = pltpu.SemaphoreType.DMA
    results = pl.pallas_call(
        kernel,
        out_shape=(
            jax.ShapeDtypeStruct((ROWS, LAT), bf16),
            jax.ShapeDtypeStruct((ROWS, LAT), bf16),
            jax.ShapeDtypeStruct((TOK, LAT), bf16),
            jax.ShapeDtypeStruct((TOK, LAT), f32),
            jax.ShapeDtypeStruct((ROPE, TOK), f32),
        ),
        in_specs=[pl.BlockSpec(memory_space=pltpu.HBM)] * 6,
        out_specs=[pl.BlockSpec(memory_space=pltpu.VMEM)] * 5,
        scratch_shapes=[
            pltpu.VMEM((ROWS, EXT), bf16),
            pltpu.VMEM((ROWS, LAT), bf16),
            pltpu.VMEM((EXT, ROWS), bf16),
            pltpu.VMEM((LAT, ROWS), bf16),
            pltpu.VMEM((KEYS, EXT), bf16),
            pltpu.VMEM((ROWS, KEYS), f32),
            pltpu.VMEM((ROWS, KEYS), f32),
            pltpu.VMEM((ROWS, TOK), f32),
            pltpu.VMEM((ROWS, KEYS), bf16),
            pltpu.VMEM((ROWS, KEYS), bf16),
            pltpu.VMEM((TOK, LAT), bf16),
            pltpu.VMEM((ROPE, TOK), bf16),
            pltpu.VMEM((1, TOK), jnp.int32),
            pltpu.VMEM((BLOCKS, EXT, TOK), bf16),
            pltpu.VMEM((BLOCKS, HALF, TOK), bf16),
            pltpu.VMEM((BLOCKS, HALF, TOK), bf16),
            pltpu.VMEM((BLOCKS, 4, PIECE, TOK), bf16),
            pltpu.VMEM((PIECE, TOK), bf16),
            pltpu.VMEM((2, PIECE, TOK), bf16),
            pltpu.VMEM((PIECE, TOK), bf16),
            pltpu.VMEM((PIECE, TOK), bf16),
            pltpu.VMEM((EXT, TOK), bf16),
            dma((6,)),
            dma, dma, dma((3,)), dma((3,)), dma((4,)), dma((4,)),
            dma((BLOCKS,)), dma((BLOCKS,)), dma((BLOCKS, 4)), dma((BLOCKS, 4)),
            dma((2,)), dma((2,)), dma, dma, dma((4,)), dma((4,)),
            pltpu.SemaphoreType.REGULAR, pltpu.SemaphoreType.REGULAR, pltpu.SemaphoreType.REGULAR,
        ],
        compiler_params=pltpu.CompilerParams(
            collective_id=0, has_side_effects=True, vmem_limit_bytes=48 * 1024 * 1024
        ),
        cost_estimate=pl.CostEstimate(
            flops=9 * 2 * ROWS * KEYS * LAT // 2, bytes_accessed=5 * 1024 * 1024,
            transcendentals=ROWS * KEYS,
        ),
    )(*[
        pltpu.with_memory_space_constraint(array, pltpu.HBM)
        for array in (
            query_latent.reshape(ROWS, LAT), query_rope, latent, key_rope.T,
            doc_ids.reshape(1, TOK), grad_out.reshape(ROWS, LAT),
        )
    ])
    attended, grad_query, grad_query_rope, grad_latent, grad_key_rope = pl.pallas_call(
        store,
        out_shape=tuple(jax.ShapeDtypeStruct(r.shape, r.dtype) for r in results),
        in_specs=[pl.BlockSpec(memory_space=pltpu.VMEM)] * 5,
        out_specs=[pl.BlockSpec(memory_space=pltpu.HBM)] * 5,
        scratch_shapes=[dma((5,))],
        compiler_params=pltpu.CompilerParams(vmem_limit_bytes=4 * 1024 * 1024),
    )(*results)
    return (
        attended.reshape(TOK, HEADS, LAT),
        grad_query.reshape(TOK, HEADS, LAT),
        grad_query_rope,
        grad_latent,
        grad_key_rope.T,
    )


def solution(mesh):
    in_specs = (
        P("ctx", "head", None),
        P("ctx", "head"),
        P("ctx", None),
        P("ctx", None),
        P("ctx"),
        P("ctx", "head", None),
    )
    out_specs = (
        P("ctx", "head", None),
        P("ctx", "head", None),
        P("ctx", "head"),
        P("ctx", None),
        P("ctx", None),
    )
    return jax.shard_map(
        per_device, mesh=mesh, in_specs=in_specs, out_specs=out_specs, check_vma=False
    )
```

time: 61.1 us -> 52.2 us (0.85)
  local copies, waits for them, and re-layouts: 9.08 us -> 0 us
    unnamed x16 -> x0, local copies, waits for them, and re-layouts: 9.08 us -> none
    pallas_call x0 -> x1, Pallas kernels: none -> 1.48 us  [per_device(): pl.pallas_call(store, out_shape=tuple((jax.ShapeDtypeStruct(r.shape, r.dt...]
    pallas_call x1, Pallas kernels: 51.1 us -> 50 us  [per_device(): pl.pallas_call(kernel, out_shape=(jax.ShapeDtypeStruct((ROWS, LAT), bf16)...]
where the time goes in v2:
time: 52.2 us; the launch traced here: 52.1 us
  Pallas kernels  51.4 us (98%)
  between operations  0.64 us (1%)
    pallas_call x1, Pallas kernels, per_device(): pl.pallas_call(kernel, out_shape=(jax.ShapeDtypeStruct((ROWS, LAT), bf16)...  50 us
    pallas_call x1, Pallas kernels, per_device(): pl.pallas_call(store, out_shape=tuple((jax.ShapeDtypeStruct(r.shape, r.dt...  1.48 us

profile of v2, /device:TPU:1, one launch (start us, length us, event | category | flops | bytes accessed | tf_op | source)
XLA Modules:
  0.0 52.1 jit_solution(7878800693784004058)
XLA Ops:
  0.6 50.0 %shard_map.101 = (bf16[1024,512]{1,0:T(8,128)(2,1)S(1)}, bf16[1024,512]{1,0:T(8,128)(2,1)S(1)}, bf16[128,512]{1,0:T(8,128)(2,1)S(1)}, f32[128,512]{1,0:T(8,128)S(1)}, f32[64,128]{1,0:T(8,128)S(1)}) custom-call(bf16[1024,512]{1,0:T(8,128)(2,1)} %bitcast.7, bf16[128,512]{1,0:T(8,128)(2,1)} %qr.1, bf16[128,512]{1,0:T(8,128)(2,1)} %lat.1, ...), custom_call_target="tpu_custom_call" | custom-call | flops 3019898880 | bytes 5242880 | tf_op jit(solution)/shard_map/pallas_call | solution.py:338
  50.6 1.5 %shard_map.102 = (bf16[1024,512]{1,0:T(8,128)(2,1)}, bf16[1024,512]{1,0:T(8,128)(2,1)}, bf16[128,512]{1,0:T(8,128)(2,1)}, f32[128,512]{1,0:T(8,128)}, f32[64,128]{1,0:T(8,128)}) custom-call(bf16[1024,512]{1,0:T(8,128)(2,1)S(1)} %get-tuple-element.15.refs_0_, bf16[1024,512]{1,0:T(8,128)(2,1)S(1)} %get-tuple-element.16.refs_1_, ...), custom_call_target="tpu_custom_call" | custom-call | tf_op jit(solution)/shard_map/pallas_call | solution.py:392

commit v3 on v2

--- a/solution.py
+++ b/solution.py
@@ -130,6 +130,8 @@
     y = lax.rem(ctx, 4)
     x = lax.rem(head // 2, 4)
     c = lax.rem(head, 2)
+    first = ctx < 4
+    last = ctx >= 28
 
     def device(dz=0, dy=0, dx=0, dc=0):
         zz = lax.rem(z + dz, 16)
@@ -144,8 +146,8 @@
             device_id=to, device_id_type=MESH,
         )
 
-    partners = [dict(dy=1), dict(dy=2), dict(dy=3), dict(dz=1), dict(dz=15), dict(dc=1)]
-    partners += [dict(dx=1), dict(dx=2), dict(dx=3)]
+    near = [dict(dy=1), dict(dy=3), dict(dz=1), dict(dz=15), dict(dx=1), dict(dx=3)]
+    partners = near + [dict(dc=1)]
     barrier = pltpu.get_barrier_semaphore()
     for partner in partners:
         pl.semaphore_signal(barrier, inc=1, device_id=device(**partner), device_id_type=MESH)
@@ -181,42 +183,79 @@
     def half(d):
         return kx.at[pl.ds(pl.multiple_of(d * TOK + c * half_rows, half_rows), half_rows)]
 
-    hz = remote(half(0), half(4), hz_s, hz_r, device(dz=1))
-    hz.start()
-
-    def hy(j, src):
-        return remote(half(src), half(j), hy_s.at[j - 1], hy_r.at[j - 1], device(dy=j))
-
-    for j in (3, 2, 1):
-        @pl.when(y + j < 4)
-        def _():
-            hy(j, 0).start()
-
-    tell(met, dict(dy=1), dict(dy=2), dict(dy=3), dict(dz=1), dict(dz=15))
+    quarter_rows = TOK // 4
+
+    def quarter(d, n):
+        start = pl.multiple_of(d * TOK + c * half_rows + n * quarter_rows, quarter_rows)
+        return kx.at[pl.ds(start, quarter_rows)]
+
+    def hz(n):
+        return remote(quarter(0, n), quarter(4, n), hz_s.at[n], hz_r.at[n], device(dz=1))
+
+    def hy(j, src, n):
+        return remote(
+            quarter(src, n), quarter(j, n), hy_s.at[j - 1, n], hy_r.at[j - 1, n], device(dy=j)
+        )
+
+    @pl.when(jnp.logical_not(last))
+    def _():
+        for n in (0, 1):
+            hz(n).start()
+
+    for n in (0, 1):
+        for j in (3, 1):
+            @pl.when(y + j < 4)
+            def _():
+                hy(j, 0, n).start()
+
+    tell(met, *near)
 
     def hc(d):
         return remote(half(d), half(d), hc_s.at[d - 1], hc_r.at[d - 1], device(dc=1))
 
-    hz.wait_recv()
-    for j in (2, 1, 3):
-        @pl.when(y + j >= 4)
-        def _():
-            hy(j, 4).start()
+    for n in (0, 1):
+        @pl.when(jnp.logical_not(first))
+        def _():
+            hz(n).wait_recv()
+            for j in (1, 3):
+                @pl.when(y + j >= 4)
+                def _():
+                    hy(j, 4, n).start()
+
+        if n == 0:
+            pl.semaphore_wait(met, len(near))
+
+        @pl.when(y < 2)
+        def _():
+            hy(2, 0, n).start()
+
+        @pl.when((y >= 2) & jnp.logical_not(first))
+        def _():
+            hy(2, 4, n).start()
+
+    for d in (1, 2, 3, 4):
+        @pl.when(first & (y < d))
+        def _():
+            half(d)[...] = jnp.full((half_rows, EXT), -1.0, jnp.bfloat16)
+
     hc(4).start()
+    tell(met_2, dict(dy=2), dict(dx=2), dict(dz=2), dict(dz=14))
 
     own_head = iota((TILE, LAT), 1) // ROPE == lax.rem(iota((TILE, LAT), 0), HEADS)
     prepare(qx, g, qxt, gt, kx, s_all, gp_all, docq, qr_v, doc_col, own_head, loads)
 
-    pl.semaphore_wait(met, 5)
-    tell(met_2, dict(dz=2), dict(dz=14))
     for j in (3, 1, 2):
-        hy(j, 0).wait_recv()
+        @pl.when(jnp.logical_not(first & (y < j)))
+        def _():
+            hy(j, 0, 0).wait_recv()
+            hy(j, 0, 1).wait_recv()
+
         hc(j).start()
     for pair in ((3, 4), (1, 2)):
         for d in pair:
             hc(d).wait_recv()
         products(qx, g, kx, s_all, gp_all, slice(pair[0] * TOK, (pair[1] + 1) * TOK))
-    pl.semaphore_wait(met_2, 2)
+    pl.semaphore_wait(met_2, 4)
     tell(met_4, dict(dz=4), dict(dz=12))
     scores(kx, s_all, gp_all, docq, p_all, gs_all)
 
@@ -283,43 +322,70 @@
     far_b = remote(b_out, b_in.at[1], zb_s.at[1], zb_r.at[1], device(dz=7))
     near_b = remote(b_out, b_in.at[0], zb_s.at[0], zb_r.at[0], device(dz=15))
     far_a = remote(a_out, a_in, zh_s, zh_r, device(dz=8))
-    far_b.start()
+
+    @pl.when(jnp.logical_not(first))
+    def _():
+        far_b.start()
+
     a = a + gathered(0)
     a_out[...] = a.astype(jnp.bfloat16)
     far_a.start()
-    near_b.start()
-
-    for copy in (near_b, far_b, far_a):
-        copy.wait_recv()
+
+    @pl.when(jnp.logical_not(first))
+    def _():
+        near_b.start()
+
+    @pl.when(last)
+    def _():
+        b_in[...] = jnp.zeros_like(b_in)
+
+    @pl.when(jnp.logical_not(last))
+    def _():
+        near_b.wait_recv()
+        far_b.wait_recv()
+
+    far_a.wait_recv()
     mine = pl.ds(pl.multiple_of(c * HALF + x * PIECE, PIECE), PIECE)
     total[mine, :] = (
         (a_out[...].astype(jnp.float32) + a_in[...].astype(jnp.float32))
         + (b_in[0].astype(jnp.float32) + b_in[1].astype(jnp.float32))
     ).astype(jnp.bfloat16)
 
-    def ag(i):
-        return remote(total.at[mine], total.at[mine], ag_s.at[i], ag_r.at[i], device(dx=i))
-
-    for i in (2, 1, 3):
-        ag(i).start()
-    for i in (2, 1, 3):
-        ag(i).wait_recv()
-    last = remote(total.at[own_half], total.at[own_half], ag_s.at[0], ag_r.at[0], device(dc=1))
-    last.start()
-    last.wait_recv()
+    def ag(i, other):
+        return remote(
+            total.at[mine], total.at[mine], ag_s.at[i, other], ag_r.at[i, other],
+            device(dx=i, dc=other),
+        )
+
+    gather = [ag(i, other) for i in (2, 1, 3, 0) for other in (1, 0) if i or other]
+    for copy in gather:
+        copy.start()
+    for copy in gather:
+        copy.wait_recv()
     gl_v[...] = dot(diagonal.astype(jnp.bfloat16), total[0:LAT, :], NT)
     gk_v[...] = total[LAT:LAT + ROPE, :].astype(jnp.float32)
 
-    hz.wait_send()
-    for j in (1, 2, 3):
-        hy(j, 0).wait_send()
+    for n in (0, 1):
+        @pl.when(jnp.logical_not(last))
+        def _():
+            hz(n).wait_send()
+
+        for j in (1, 2, 3):
+            @pl.when(jnp.logical_not(first & (y + j >= 4)))
+            def _():
+                hy(j, 0, n).wait_send()
     for d in (1, 2, 3, 4):
         hc(d).wait_send()
     for d in range(BLOCKS):
         core_sum(d).wait_send()
         for i in remote_pieces(d):
             xy(d, i).wait_send()
-    for copy in (near_b, far_b, far_a, ag(1), ag(2), ag(3), last):
+    @pl.when(jnp.logical_not(first))
+    def _():
+        near_b.wait_send()
+        far_b.wait_send()
+
+    for copy in [far_a] + gather:
         copy.wait_send()
 
 
@@ -370,9 +436,9 @@
             pltpu.VMEM((PIECE, TOK), bf16),
             pltpu.VMEM((EXT, TOK), bf16),
             dma((6,)),
-            dma, dma, dma((3,)), dma((3,)), dma((4,)), dma((4,)),
+            dma((2,)), dma((2,)), dma((3, 2)), dma((3, 2)), dma((4,)), dma((4,)),
             dma((BLOCKS,)), dma((BLOCKS,)), dma((BLOCKS, 4)), dma((BLOCKS, 4)),
-            dma((2,)), dma((2,)), dma, dma, dma((4,)), dma((4,)),
+            dma((2,)), dma((2,)), dma, dma, dma((4, 2)), dma((4, 2)),
             pltpu.SemaphoreType.REGULAR, pltpu.SemaphoreType.REGULAR, pltpu.SemaphoreType.REGULAR,
         ],
         compiler_params=pltpu.CompilerParams(

time: 52.2 us -> 50 us (0.958)
  Pallas kernels: 51.4 us -> 49.3 us
    pallas_call x1, Pallas kernels: 50 us -> 47.8 us  [per_device(): pl.pallas_call(kernel, out_shape=(jax.ShapeDtypeStruct((ROWS, LAT), bf16)...]
where the time goes in v3:
time: 50 us; the launch traced here: 49.9 us
  Pallas kernels  49.3 us (99%)
  between operations  0.64 us (1%)
    pallas_call x1, Pallas kernels, per_device(): pl.pallas_call(kernel, out_shape=(jax.ShapeDtypeStruct((ROWS, LAT), bf16)...  47.8 us
    pallas_call x1, Pallas kernels, per_device(): pl.pallas_call(store, out_shape=tuple((jax.ShapeDtypeStruct(r.shape, r.dt...  1.48 us

profile of v3, /device:TPU:1, one launch (start us, length us, event | category | flops | bytes accessed | tf_op | source)
XLA Modules:
  0.0 49.9 jit_solution(9518510344728754127)
XLA Ops:
  0.6 47.8 %shard_map.101 = (bf16[1024,512]{1,0:T(8,128)(2,1)S(1)}, bf16[1024,512]{1,0:T(8,128)(2,1)S(1)}, bf16[128,512]{1,0:T(8,128)(2,1)S(1)}, f32[128,512]{1,0:T(8,128)S(1)}, f32[64,128]{1,0:T(8,128)S(1)}) custom-call(bf16[1024,512]{1,0:T(8,128)(2,1)} %bitcast.7, bf16[128,512]{1,0:T(8,128)(2,1)} %qr.1, bf16[128,512]{1,0:T(8,128)(2,1)} %lat.1, ...), custom_call_target="tpu_custom_call" | custom-call | flops 3019898880 | bytes 5242880 | tf_op jit(solution)/shard_map/pallas_call | solution.py:404
  48.4 1.5 %shard_map.102 = (bf16[1024,512]{1,0:T(8,128)(2,1)}, bf16[1024,512]{1,0:T(8,128)(2,1)}, bf16[128,512]{1,0:T(8,128)(2,1)}, f32[128,512]{1,0:T(8,128)}, f32[64,128]{1,0:T(8,128)}) custom-call(bf16[1024,512]{1,0:T(8,128)(2,1)S(1)} %get-tuple-element.15.refs_0_, bf16[1024,512]{1,0:T(8,128)(2,1)S(1)} %get-tuple-element.16.refs_1_, ...), custom_call_target="tpu_custom_call" | custom-call | tf_op jit(solution)/shard_map/pallas_call | solution.py:458

commit v4 on v3

--- a/solution.py
+++ b/solution.py
@@ -20,8 +20,12 @@
 EXT = 640
 BLOCKS = 5
 KEYS = TOK * BLOCKS
-HALF = EXT // 2
-PIECE = HALF // 4
+FEATURES = LAT + ROPE
+START = (0, 320)
+SPAN = (320, 256)
+PIECE = (80, 64)
+PLACES = [(64 * n, 64, 80 * n) for n in range(4)] + [(256, 128, 320), (384, 128, 448)]
+PLACES += [(LAT + 16 * n, 16, 80 * n + 64) for n in range(4)]
 NT = (((1,), (1,)), ((), ()))
 NN = (((1,), (0,)), ((), ()))
 TILE = 256
@@ -36,8 +40,8 @@
     return lax.broadcasted_iota(jnp.int32, shape, dim)
 
 
-def products(qx, g, kx, s_all, gp_all, keys):
-    for r in range(0, ROWS, TILE):
+def products(qx, g, kx, s_all, gp_all, keys, tiles=range(0, ROWS, TILE)):
+    for r in tiles:
         s_all[r:r + TILE, keys] = dot(qx[r:r + TILE, :], kx[keys, :], NT)
         gp_all[r:r + TILE, keys] = dot(g[r:r + TILE, :], kx[keys, 0:LAT], NT)
 
@@ -62,45 +66,54 @@
         gt[:, r:r + TILE] = g[r:r + TILE, :].T
 
 
-def scores(kx, s_all, gp_all, docq, p_all, gs_all):
-    pick = (iota((8, 128), 1) == ROPE).astype(jnp.bfloat16)
-    docs = [dot(pick, kx[d * TOK:(d + 1) * TOK, LAT:EXT], NT)[0:1] for d in range(BLOCKS)]
-    for r in range(0, ROWS, TILE):
-        for q in range(r, r + TILE, CHUNK):
-            rows = slice(q, q + CHUNK)
-            doc_here = docq[rows, :]
-            causal = q // HEADS + iota((CHUNK, TOK), 0) // HEADS >= iota((CHUNK, TOK), 1)
-            score = []
-            for d in range(BLOCKS):
-                allowed = doc_here == docs[d]
-                if d == 0:
-                    allowed = allowed & causal
-                score.append(jnp.where(allowed, s_all[rows, d * TOK:(d + 1) * TOK], NEGATIVE))
-            most = functools.reduce(jnp.maximum, score)
-            most = jnp.max(most, axis=1, keepdims=True) * (SCORE_SCALE * LOG2E)
-            weight = [jnp.exp2(tile * (SCORE_SCALE * LOG2E) - most) for tile in score]
-            gp = [gp_all[rows, d * TOK:(d + 1) * TOK] for d in range(BLOCKS)]
-            norm = jnp.sum(functools.reduce(jnp.add, weight), axis=1, keepdims=True)
-            delta = functools.reduce(jnp.add, [w * t for w, t in zip(weight, gp)])
-            delta = jnp.sum(delta, axis=1, keepdims=True)
-            inverse = 1.0 / norm
-            delta = delta * inverse
-            for d in range(BLOCKS):
-                prob = weight[d] * inverse
-                p_all[rows, d * TOK:(d + 1) * TOK] = prob.astype(jnp.bfloat16)
-                gs_all[rows, d * TOK:(d + 1) * TOK] = (
-                    (SCORE_SCALE * prob) * (gp[d] - delta)
-                ).astype(jnp.bfloat16)
-
-
-def key_grads(qxt, gt, gs_all, p_all, part, group):
+def scores(r, docs, s_all, gp_all, docq, p_all, gs_all):
+    rows = slice(r, r + CHUNK)
+    doc_here = docq[rows, :]
+    causal = r // HEADS + iota((CHUNK, TOK), 0) // HEADS >= iota((CHUNK, TOK), 1)
+    score = []
+    for d in range(BLOCKS):
+        allowed = doc_here == docs[d]
+        if d == 0:
+            allowed = allowed & causal
+        score.append(jnp.where(allowed, s_all[rows, d * TOK:(d + 1) * TOK], NEGATIVE))
+    most = functools.reduce(jnp.maximum, score)
+    most = jnp.max(most, axis=1, keepdims=True) * (SCORE_SCALE * LOG2E)
+    weight = [jnp.exp2(tile * (SCORE_SCALE * LOG2E) - most) for tile in score]
+    gp = [gp_all[rows, d * TOK:(d + 1) * TOK] for d in range(BLOCKS)]
+    norm = jnp.sum(functools.reduce(jnp.add, weight), axis=1, keepdims=True)
+    delta = functools.reduce(jnp.add, [w * t for w, t in zip(weight, gp)])
+    delta = jnp.sum(delta, axis=1, keepdims=True)
+    inverse = 1.0 / norm
+    delta = delta * inverse
+    for d in range(BLOCKS):
+        prob = weight[d] * inverse
+        p_all[rows, d * TOK:(d + 1) * TOK] = prob.astype(jnp.bfloat16)
+        gs_all[rows, d * TOK:(d + 1) * TOK] = (
+            (SCORE_SCALE * prob) * (gp[d] - delta)
+        ).astype(jnp.bfloat16)
+
+
+GROUPS = ((1, 2), (3, 4), (0,))
+
+
+def key_sum(qxt, gt, gs_all, p_all, f, group, rows):
     cols = slice(group[0] * TOK, (group[-1] + 1) * TOK)
+    grads = dot(qxt[f:f + 128, rows], gs_all[rows, cols])
+    if f < LAT:
+        grads = grads + dot(gt[f:f + 128, rows], p_all[rows, cols])
+    return grads
+
+
+def key_grads(qxt, gt, gs_all, p_all, acc, part, group):
     for f in range(0, EXT, 128):
-        grads = dot(qxt[f:f + 128, :], gs_all[:, cols])
-        if f < LAT:
-            grads = grads + dot(gt[f:f + 128, :], p_all[:, cols])
+        grads = key_sum(qxt, gt, gs_all, p_all, f, group, slice(ROWS // 2, ROWS))
         for k, d in enumerate(group):
-            part[d, f:f + 128, :] = grads[:, k * TOK:(k + 1) * TOK].astype(jnp.bfloat16)
+            block = (
+                grads[:, k * TOK:(k + 1) * TOK] + acc[f:f + 128, d * TOK:(d + 1) * TOK]
+            ).astype(jnp.bfloat16)
+            for start, rows, to in PLACES:
+                if f <= start < f + 128:
+                    part[d, to:to + rows, :] = block[start - f:start - f + rows]
 
 
 def outputs(p_all, gs_all, kx, own_head, o_v, dq_v, dqr_v, r):
@@ -118,7 +131,7 @@
 def kernel(
     ql, qr, lat, kr, doc, go,
     o_v, dq_v, dqr_v, gl_v, gk_v,
-    qx, g, qxt, gt, kx, s_all, gp_all, docq, p_all, gs_all,
+    qx, g, qxt, gt, kx, s_all, gp_all, docq, p_all, gs_all, acc,
     qr_v, kr_v, doc_v,
     part, part_in, summed, pieces_in, b_out, b_in, a_out, a_in, total,
     in_sem, hz_s, hz_r, hy_s, hy_r, hc_s, hc_r,
@@ -214,25 +227,21 @@
         return remote(half(d), half(d), hc_s.at[d - 1], hc_r.at[d - 1], device(dc=1))
 
     for n in (0, 1):
+        if n == 0:
+            pl.semaphore_wait(met, len(near))
+
+        @pl.when(y < 2)
+        def _():
+            hy(2, 0, n).start()
+
         @pl.when(jnp.logical_not(first))
         def _():
             hz(n).wait_recv()
-            for j in (1, 3):
+            for j in (2, 1, 3):
                 @pl.when(y + j >= 4)
                 def _():
                     hy(j, 4, n).start()
 
-        if n == 0:
-            pl.semaphore_wait(met, len(near))
-
-        @pl.when(y < 2)
-        def _():
-            hy(2, 0, n).start()
-
-        @pl.when((y >= 2) & jnp.logical_not(first))
-        def _():
-            hy(2, 4, n).start()
-
     for d in (1, 2, 3, 4):
         @pl.when(first & (y < d))
         def _():
@@ -251,119 +260,156 @@
             hy(j, 0, 1).wait_recv()
 
         hc(j).start()
-    for pair in ((3, 4), (1, 2)):
-        for d in pair:
-            hc(d).wait_recv()
-        products(qx, g, kx, s_all, gp_all, slice(pair[0] * TOK, (pair[1] + 1) * TOK))
+    hc(3).wait_recv()
+    hc(4).wait_recv()
+    products(qx, g, kx, s_all, gp_all, slice(3 * TOK, 5 * TOK))
     pl.semaphore_wait(met_2, 4)
     tell(met_4, dict(dz=4), dict(dz=12))
-    scores(kx, s_all, gp_all, docq, p_all, gs_all)
-
-    own_half = pl.ds(pl.multiple_of(c * HALF, HALF), HALF)
-    other_half = pl.ds(pl.multiple_of((1 - c) * HALF, HALF), HALF)
-
-    def core_sum(d):
+    hc(1).wait_recv()
+    hc(2).wait_recv()
+    pick = (iota((8, 128), 1) == ROPE).astype(jnp.bfloat16)
+    docs = [dot(pick, kx[d * TOK:(d + 1) * TOK, LAT:EXT], NT)[0:1] for d in range(BLOCKS)]
+    beside = [(f, group) for group in GROUPS for f in range(0, EXT, 128)]
+    products(qx, g, kx, s_all, gp_all, slice(TOK, 3 * TOK), [0])
+    for r in range(0, ROWS, CHUNK):
+        if r % TILE == 0 and r + TILE < ROWS:
+            products(qx, g, kx, s_all, gp_all, slice(TOK, 3 * TOK), [r + TILE])
+        scores(r, docs, s_all, gp_all, docq, p_all, gs_all)
+        if r >= ROWS // 2:
+            for f, group in beside[:2]:
+                cols = slice(group[0] * TOK, (group[-1] + 1) * TOK)
+                acc[f:f + 128, cols] = key_sum(
+                    qxt, gt, gs_all, p_all, f, group, slice(0, ROWS // 2)
+                )
+            beside = beside[2:]
+
+    def by_core(step):
+        for own in (0, 1):
+            pl.when(c == own)(functools.partial(step, own))
+
+    def core_sum(d, giver):
+        other = 1 - giver
         return remote(
-            part.at[d, other_half], part_in.at[d], cs_s.at[d], cs_r.at[d], device(dc=1)
-        )
-
-    def xy(d, i):
+            part.at[d, pl.ds(START[other], SPAN[other])], part_in.at[d, pl.ds(0, SPAN[other])],
+            cs_s.at[d], cs_r.at[d], device(dc=1),
+        )
+
+    def piece(own, place):
+        return pl.ds(pl.multiple_of(place * PIECE[own], PIECE[own]), PIECE[own])
+
+    def xy(d, i, own):
         to = device(dx=i) if d in (0, 4) else device(dx=i, dy=4 - d)
-        here = pl.ds(pl.multiple_of(lax.rem(x + i, 4) * PIECE, PIECE), PIECE)
         return remote(
-            summed.at[d, here], pieces_in.at[d, i], xy_s.at[d, i], xy_r.at[d, i], to
+            summed.at[d, piece(own, lax.rem(x + i, 4))], pieces_in.at[d, i, pl.ds(0, PIECE[own])],
+            xy_s.at[d, i], xy_r.at[d, i], to,
         )
 
     def remote_pieces(d):
         return [i for i in (2, 1, 3, 0) if d not in (0, 4) or i]
 
-    def pass_on(d):
-        core_sum(d).wait_recv()
-        summed[d] = (
-            part[d, own_half].astype(jnp.float32) + part_in[d].astype(jnp.float32)
-        ).astype(jnp.bfloat16)
-        for i in remote_pieces(d):
-            xy(d, i).start()
-
-    groups = [(1, 2), (3, 4), (0,)]
-    for n, group in enumerate(groups):
-        key_grads(qxt, gt, gs_all, p_all, part, group)
+    def pass_on(group, own):
         for d in group:
-            core_sum(d).start()
+            core_sum(d, 1 - own).wait_recv()
+            summed[d, 0:SPAN[own]] = (
+                part[d, START[own]:START[own] + SPAN[own]].astype(jnp.float32)
+                + part_in[d, 0:SPAN[own]].astype(jnp.float32)
+            ).astype(jnp.bfloat16)
+            for i in remote_pieces(d):
+                xy(d, i, own).start()
+
+    def exchange(group, own):
+        for d in group:
+            core_sum(d, own).start()
+
+    for n, group in enumerate(GROUPS):
+        key_grads(qxt, gt, gs_all, p_all, acc, part, group)
+        by_core(functools.partial(exchange, group))
         if n:
-            for d in groups[n - 1]:
-                pass_on(d)
+            by_core(functools.partial(pass_on, GROUPS[n - 1]))
 
     outputs(p_all, gs_all, kx, own_head, o_v, dq_v, dqr_v, 0)
-    for d in groups[-1]:
-        pass_on(d)
+    by_core(functools.partial(pass_on, GROUPS[-1]))
     for r in range(TILE, ROWS, TILE):
         outputs(p_all, gs_all, kx, own_head, o_v, dq_v, dqr_v, r)
 
-    own_piece = pl.ds(pl.multiple_of(x * PIECE, PIECE), PIECE)
-
-    def gathered(d):
-        terms = [] if d in range(1, 4) else [summed[d, own_piece].astype(jnp.float32)]
-        for i in remote_pieces(d):
-            xy(d, i).wait_recv()
-            terms.append(pieces_in[d, i].astype(jnp.float32))
-        return functools.reduce(jnp.add, terms)
-
-    b = jnp.zeros((PIECE, TOK), jnp.float32)
-    a = jnp.zeros((PIECE, TOK), jnp.float32)
-    for d in (1, 2, 3):
-        term = gathered(d)
-        same = y + d < 4
-        a = a + jnp.where(same, term, 0.0)
-        b = b + jnp.where(same, 0.0, term)
-    b = b + gathered(4)
-    b_out[...] = b.astype(jnp.bfloat16)
-    pl.semaphore_wait(met_4, 2)
-    far_b = remote(b_out, b_in.at[1], zb_s.at[1], zb_r.at[1], device(dz=7))
-    near_b = remote(b_out, b_in.at[0], zb_s.at[0], zb_r.at[0], device(dz=15))
-    far_a = remote(a_out, a_in, zh_s, zh_r, device(dz=8))
-
-    @pl.when(jnp.logical_not(first))
-    def _():
-        far_b.start()
-
-    a = a + gathered(0)
-    a_out[...] = a.astype(jnp.bfloat16)
-    far_a.start()
-
-    @pl.when(jnp.logical_not(first))
-    def _():
-        near_b.start()
-
-    @pl.when(last)
-    def _():
-        b_in[...] = jnp.zeros_like(b_in)
-
-    @pl.when(jnp.logical_not(last))
-    def _():
-        near_b.wait_recv()
-        far_b.wait_recv()
-
-    far_a.wait_recv()
-    mine = pl.ds(pl.multiple_of(c * HALF + x * PIECE, PIECE), PIECE)
-    total[mine, :] = (
-        (a_out[...].astype(jnp.float32) + a_in[...].astype(jnp.float32))
-        + (b_in[0].astype(jnp.float32) + b_in[1].astype(jnp.float32))
-    ).astype(jnp.bfloat16)
-
-    def ag(i, other):
+    def far_copies(own):
+        rows = pl.ds(0, PIECE[own])
+        return (
+            remote(b_out.at[rows], b_in.at[0, rows], zb_s.at[0], zb_r.at[0], device(dz=15)),
+            remote(b_out.at[rows], b_in.at[1, rows], zb_s.at[1], zb_r.at[1], device(dz=7)),
+            remote(a_out.at[rows], a_in.at[rows], zh_s, zh_r, device(dz=8)),
+        )
+
+    def ag(i, other, giver):
+        rows = pl.ds(pl.multiple_of(START[giver] + x * PIECE[giver], 16), PIECE[giver])
         return remote(
-            total.at[mine], total.at[mine], ag_s.at[i, other], ag_r.at[i, other],
+            total.at[rows], total.at[rows], ag_s.at[i, other], ag_r.at[i, other],
             device(dx=i, dc=other),
         )
 
-    gather = [ag(i, other) for i in (2, 1, 3, 0) for other in (1, 0) if i or other]
-    for copy in gather:
-        copy.start()
-    for copy in gather:
-        copy.wait_recv()
-    gl_v[...] = dot(diagonal.astype(jnp.bfloat16), total[0:LAT, :], NT)
-    gk_v[...] = total[LAT:LAT + ROPE, :].astype(jnp.float32)
+    spread = [(i, other) for i in (2, 1, 3, 0) for other in (1, 0) if i or other]
+
+    def finish(own):
+        rows = PIECE[own]
+
+        def gathered(d):
+            terms = []
+            if d in (0, 4):
+                terms.append(summed[d, piece(own, x)].astype(jnp.float32))
+            for i in remote_pieces(d):
+                xy(d, i, own).wait_recv()
+                terms.append(pieces_in[d, i, 0:rows].astype(jnp.float32))
+            return functools.reduce(jnp.add, terms)
+
+        b = jnp.zeros((rows, TOK), jnp.float32)
+        a = jnp.zeros((rows, TOK), jnp.float32)
+        for d in (1, 2, 3):
+            term = gathered(d)
+            same = y + d < 4
+            a = a + jnp.where(same, term, 0.0)
+            b = b + jnp.where(same, 0.0, term)
+        b = b + gathered(4)
+        b_out[0:rows] = b.astype(jnp.bfloat16)
+        pl.semaphore_wait(met_4, 2)
+        near_b, far_b, far_a = far_copies(own)
+
+        @pl.when(jnp.logical_not(first))
+        def _():
+            far_b.start()
+
+        a = a + gathered(0)
+        a_out[0:rows] = a.astype(jnp.bfloat16)
+        far_a.start()
+
+        @pl.when(jnp.logical_not(first))
+        def _():
+            near_b.start()
+
+        @pl.when(last)
+        def _():
+            b_in[...] = jnp.zeros_like(b_in)
+
+        @pl.when(jnp.logical_not(last))
+        def _():
+            near_b.wait_recv()
+            far_b.wait_recv()
+
+        far_a.wait_recv()
+        mine = pl.ds(pl.multiple_of(START[own] + x * rows, 16), rows)
+        total[mine, :] = (
+            (a_out[0:rows].astype(jnp.float32) + a_in[0:rows].astype(jnp.float32))
+            + (b_in[0, 0:rows].astype(jnp.float32) + b_in[1, 0:rows].astype(jnp.float32))
+        ).astype(jnp.bfloat16)
+        for i, other in spread:
+            ag(i, other, own).start()
+        for i, other in spread:
+            ag(i, other, (own + other) % 2).wait_recv()
+
+    by_core(finish)
+    latent_rows = [total[to:to + rows, :] for start, rows, to in PLACES if start < LAT]
+    rope_rows = [total[to:to + rows, :] for start, rows, to in PLACES if start >= LAT]
+    gl_v[...] = dot(diagonal.astype(jnp.bfloat16), jnp.concatenate(latent_rows, axis=0), NT)
+    gk_v[...] = jnp.concatenate(rope_rows, axis=0).astype(jnp.float32)
 
     for n in (0, 1):
         @pl.when(jnp.logical_not(last))
@@ -376,17 +422,24 @@
                 hy(j, 0, n).wait_send()
     for d in (1, 2, 3, 4):
         hc(d).wait_send()
-    for d in range(BLOCKS):
-        core_sum(d).wait_send()
-        for i in remote_pieces(d):
-            xy(d, i).wait_send()
-    @pl.when(jnp.logical_not(first))
-    def _():
-        near_b.wait_send()
-        far_b.wait_send()
-
-    for copy in [far_a] + gather:
-        copy.wait_send()
+
+    def sent(own):
+        for d in range(BLOCKS):
+            core_sum(d, own).wait_send()
+            for i in remote_pieces(d):
+                xy(d, i, own).wait_send()
+        near_b, far_b, far_a = far_copies(own)
+
+        @pl.when(jnp.logical_not(first))
+        def _():
+            near_b.wait_send()
+            far_b.wait_send()
+
+        far_a.wait_send()
+        for i, other in spread:
+            ag(i, other, own).wait_send()
+
+    by_core(sent)
 
 
 def store(*refs):
@@ -423,18 +476,19 @@
             pltpu.VMEM((ROWS, TOK), f32),
             pltpu.VMEM((ROWS, KEYS), bf16),
             pltpu.VMEM((ROWS, KEYS), bf16),
+            pltpu.VMEM((EXT, KEYS), f32),
             pltpu.VMEM((TOK, LAT), bf16),
             pltpu.VMEM((ROPE, TOK), bf16),
             pltpu.VMEM((1, TOK), jnp.int32),
-            pltpu.VMEM((BLOCKS, EXT, TOK), bf16),
-            pltpu.VMEM((BLOCKS, HALF, TOK), bf16),
-            pltpu.VMEM((BLOCKS, HALF, TOK), bf16),
-            pltpu.VMEM((BLOCKS, 4, PIECE, TOK), bf16),
-            pltpu.VMEM((PIECE, TOK), bf16),
-            pltpu.VMEM((2, PIECE, TOK), bf16),
-            pltpu.VMEM((PIECE, TOK), bf16),
-            pltpu.VMEM((PIECE, TOK), bf16),
-            pltpu.VMEM((EXT, TOK), bf16),
+            pltpu.VMEM((BLOCKS, FEATURES, TOK), bf16),
+            pltpu.VMEM((BLOCKS, SPAN[0], TOK), bf16),
+            pltpu.VMEM((BLOCKS, SPAN[0], TOK), bf16),
+            pltpu.VMEM((BLOCKS, 4, PIECE[0], TOK), bf16),
+            pltpu.VMEM((PIECE[0], TOK), bf16),
+            pltpu.VMEM((2, PIECE[0], TOK), bf16),
+            pltpu.VMEM((PIECE[0], TOK), bf16),
+            pltpu.VMEM((PIECE[0], TOK), bf16),
+            pltpu.VMEM((FEATURES, TOK), bf16),
             dma((6,)),
             dma((2,)), dma((2,)), dma((3, 2)), dma((3, 2)), dma((4,)), dma((4,)),
             dma((BLOCKS,)), dma((BLOCKS,)), dma((BLOCKS, 4)), dma((BLOCKS, 4)),

time: 50 us -> 48.4 us (0.968)
  Pallas kernels: 49.3 us -> 47.6 us
    pallas_call x1, Pallas kernels: 47.8 us -> 46.1 us  [per_device(): pl.pallas_call(kernel, out_shape=(jax.ShapeDtypeStruct((ROWS, LAT), bf16)...]
where the time goes in v4:
time: 48.4 us; the launch traced here: 48.3 us
  Pallas kernels  47.6 us (98%)
  between operations  0.64 us (1%)
    pallas_call x1, Pallas kernels, per_device(): pl.pallas_call(kernel, out_shape=(jax.ShapeDtypeStruct((ROWS, LAT), bf16)...  46.1 us
    pallas_call x1, Pallas kernels, per_device(): pl.pallas_call(store, out_shape=tuple((jax.ShapeDtypeStruct(r.shape, r.dt...  1.48 us

profile of v4, /device:TPU:1, one launch (start us, length us, event | category | flops | bytes accessed | tf_op | source)
XLA Modules:
  0.0 48.3 jit_solution(15610575450948059661)
XLA Ops:
  0.6 46.1 %shard_map.101 = (bf16[1024,512]{1,0:T(8,128)(2,1)S(1)}, bf16[1024,512]{1,0:T(8,128)(2,1)S(1)}, bf16[128,512]{1,0:T(8,128)(2,1)S(1)}, f32[128,512]{1,0:T(8,128)S(1)}, f32[64,128]{1,0:T(8,128)S(1)}) custom-call(bf16[1024,512]{1,0:T(8,128)(2,1)} %bitcast.7, bf16[128,512]{1,0:T(8,128)(2,1)} %qr.1, bf16[128,512]{1,0:T(8,128)(2,1)} %lat.1, ...), custom_call_target="tpu_custom_call" | custom-call | flops 3019898880 | bytes 5242880 | tf_op jit(solution)/shard_map/pallas_call | solution.py:457
  46.8 1.5 %shard_map.102 = (bf16[1024,512]{1,0:T(8,128)(2,1)}, bf16[1024,512]{1,0:T(8,128)(2,1)}, bf16[128,512]{1,0:T(8,128)(2,1)}, f32[128,512]{1,0:T(8,128)}, f32[64,128]{1,0:T(8,128)}) custom-call(bf16[1024,512]{1,0:T(8,128)(2,1)S(1)} %get-tuple-element.15.refs_0_, bf16[1024,512]{1,0:T(8,128)(2,1)S(1)} %get-tuple-element.16.refs_1_, ...), custom_call_target="tpu_custom_call" | custom-call | tf_op jit(solution)/shard_map/pallas_call | solution.py:512

commit v5 on v4

--- a/solution.py
+++ b/solution.py
@@ -70,27 +70,31 @@
     rows = slice(r, r + CHUNK)
     doc_here = docq[rows, :]
     causal = r // HEADS + iota((CHUNK, TOK), 0) // HEADS >= iota((CHUNK, TOK), 1)
-    score = []
-    for d in range(BLOCKS):
-        allowed = doc_here == docs[d]
-        if d == 0:
-            allowed = allowed & causal
-        score.append(jnp.where(allowed, s_all[rows, d * TOK:(d + 1) * TOK], NEGATIVE))
+
+    def tile(ref, d):
+        return ref[rows, d * TOK:(d + 1) * TOK]
+
+    docs = [jnp.where(causal, docs[0], docs[4])] + docs[1:4]
+    score = [jnp.where(causal, tile(s_all, 0), tile(s_all, 4))] + [tile(s_all, d) for d in (1, 2, 3)]
+    gp = [jnp.where(causal, tile(gp_all, 0), tile(gp_all, 4))] + [tile(gp_all, d) for d in (1, 2, 3)]
+    score = [jnp.where(doc_here == docs[n], score[n], NEGATIVE) for n in range(4)]
     most = functools.reduce(jnp.maximum, score)
     most = jnp.max(most, axis=1, keepdims=True) * (SCORE_SCALE * LOG2E)
-    weight = [jnp.exp2(tile * (SCORE_SCALE * LOG2E) - most) for tile in score]
-    gp = [gp_all[rows, d * TOK:(d + 1) * TOK] for d in range(BLOCKS)]
+    weight = [jnp.exp2(part * (SCORE_SCALE * LOG2E) - most) for part in score]
     norm = jnp.sum(functools.reduce(jnp.add, weight), axis=1, keepdims=True)
     delta = functools.reduce(jnp.add, [w * t for w, t in zip(weight, gp)])
     delta = jnp.sum(delta, axis=1, keepdims=True)
     inverse = 1.0 / norm
     delta = delta * inverse
-    for d in range(BLOCKS):
-        prob = weight[d] * inverse
-        p_all[rows, d * TOK:(d + 1) * TOK] = prob.astype(jnp.bfloat16)
-        gs_all[rows, d * TOK:(d + 1) * TOK] = (
-            (SCORE_SCALE * prob) * (gp[d] - delta)
-        ).astype(jnp.bfloat16)
+    for n in range(4):
+        prob = weight[n] * inverse
+        grad = (SCORE_SCALE * prob) * (gp[n] - delta)
+        for ref, value in ((p_all, prob), (gs_all, grad)):
+            if n:
+                ref[rows, n * TOK:(n + 1) * TOK] = value.astype(jnp.bfloat16)
+            else:
+                ref[rows, 0:TOK] = jnp.where(causal, value, 0.0).astype(jnp.bfloat16)
+                ref[rows, 4 * TOK:5 * TOK] = jnp.where(causal, 0.0, value).astype(jnp.bfloat16)
 
 
 GROUPS = ((1, 2), (3, 4), (0,))

time: 48.4 us -> 48.4 us (level)
  no operation moved by 1% of the time
where the time goes in v5:
time: 48.4 us; the launch traced here: 48.2 us
  Pallas kernels  47.6 us (98%)
  between operations  0.64 us (1%)
    pallas_call x1, Pallas kernels, per_device(): pl.pallas_call(kernel, out_shape=(jax.ShapeDtypeStruct((ROWS, LAT), bf16)...  46.1 us
    pallas_call x1, Pallas kernels, per_device(): pl.pallas_call(store, out_shape=tuple((jax.ShapeDtypeStruct(r.shape, r.dt...  1.48 us

profile of v5, /device:TPU:1, one launch (start us, length us, event | category | flops | bytes accessed | tf_op | source)
XLA Modules:
  0.0 48.2 jit_solution(17211084538935188013)
XLA Ops:
  0.6 46.1 %shard_map.101 = (bf16[1024,512]{1,0:T(8,128)(2,1)S(1)}, bf16[1024,512]{1,0:T(8,128)(2,1)S(1)}, bf16[128,512]{1,0:T(8,128)(2,1)S(1)}, f32[128,512]{1,0:T(8,128)S(1)}, f32[64,128]{1,0:T(8,128)S(1)}) custom-call(bf16[1024,512]{1,0:T(8,128)(2,1)} %bitcast.7, bf16[128,512]{1,0:T(8,128)(2,1)} %qr.1, bf16[128,512]{1,0:T(8,128)(2,1)} %lat.1, ...), custom_call_target="tpu_custom_call" | custom-call | flops 3019898880 | bytes 5242880 | tf_op jit(solution)/shard_map/pallas_call | solution.py:461
  46.7 1.5 %shard_map.102 = (bf16[1024,512]{1,0:T(8,128)(2,1)}, bf16[1024,512]{1,0:T(8,128)(2,1)}, bf16[128,512]{1,0:T(8,128)(2,1)}, f32[128,512]{1,0:T(8,128)}, f32[64,128]{1,0:T(8,128)}) custom-call(bf16[1024,512]{1,0:T(8,128)(2,1)S(1)} %get-tuple-element.15.refs_0_, bf16[1024,512]{1,0:T(8,128)(2,1)S(1)} %get-tuple-element.16.refs_1_, ...), custom_call_target="tpu_custom_call" | custom-call | tf_op jit(solution)/shard_map/pallas_call | solution.py:516
